TPU v7x, 256 devices: a whole 4x4x8 slice. The times are simulated.
256 devices in a mesh: blk: 128 (over x, y_hi, z, core), grp: 2 (over y_lo).
Axes of the slice: x: 4, y: 4 (y_hi: 2, y_lo: 2; y = y_hi * 2 + y_lo), z: 8, core: 2. Of those that a mesh axis runs over, the one named last changes fastest.
Arguments:
- rows: float32 [2048, 1024], P(('blk', 'grp')), may hold values from -6 to 6
- lognorm: float32 [2048], P(('blk', 'grp')), may hold values from 3.5 to 5.5
- centroids: float32 [131072, 1024], P('blk'), may hold values from -0.1875 to 0.1875
- counts: int32 [131072], P('blk'), may hold values from 0 to 4096
Outputs:
- numerator: float32 [131072, 1024], P('blk')
- weights: float32 [131072], P('blk')
All inputs are finite; a program needn't handle non-finite values.
Results may differ from a plain program's by a relative error of at most 0.0003.
Values sent between devices are 32-bit elements; how exact they have to be, the bound alone decides.
No kernel may reach another device: no remote copies, remote signals or barrier semaphores. Data moves between devices by JAX's collectives and lax.ppermute only.
A program may use at most 64 MiB of HBM per device.

v0:
```python
import jax
import jax.numpy as jnp
from jax import lax
from jax.sharding import PartitionSpec as P


def make_update(shard, penalty, piece):
    part_rows, part_norm = piece
    score = jnp.dot(
        part_rows, shard.T, precision=lax.Precision.HIGHEST, preferred_element_type=jnp.float32
    )
    resp = jnp.exp(score - penalty[None, :] - part_norm[:, None])
    total = jnp.dot(
        resp.T, part_rows, precision=lax.Precision.HIGHEST, preferred_element_type=jnp.float32
    )
    return (total, jnp.sum(resp, axis=0))


def body(rows, lognorm, centroids, counts):
    penalty = 0.5 * jnp.log1p(counts.astype(jnp.float32))
    partial_num, partial_mass = make_update(
        centroids,
        penalty,
        (
            lax.all_gather(rows, "blk", axis=0, tiled=True),
            lax.all_gather(lognorm, "blk", axis=0, tiled=True),
        ),
    )
    numerator, weights = lax.psum((partial_num, partial_mass), "grp")
    return (numerator, weights)


def solution(mesh):
    in_specs = (P(("blk", "grp"), None), P(("blk", "grp")), P("blk", None), P("blk"))
    out_specs = (P("blk", None), P("blk"))
    return jax.shard_map(body, mesh=mesh, in_specs=in_specs, out_specs=out_specs, check_vma=False)
```

profile of v0, /device:TPU:1, one launch (start us, length us, event | category | flops | bytes accessed | tf_op | source)
XLA Modules:
  0.0 503.6 jit_solution(18249048303555450864)
XLA Ops:
  7.2 0.0 all-gather.2.cloned.1.call-start
  7.2 0.7 all-gather.2.cloned.1.call-update
  7.9 0.0 all-reduce.3.cloned.1.call-start
  7.9 1.3 dynamic-slice
  9.9 0.9 dynamic-update-slice
  10.7 328.3 %all-reduce = f32[1024]{0:T(1024)S(1)} all-reduce(f32[1024]{0:T(1024)S(1)} %dynamic-update-slice), channel_id=1, replica_groups=mesh['blk'=128,'grp'=2] {'blk'}, use_global_device_ids=true, to_apply=%add | all-reduce | flops 1024 | bytes 8192
  339.1 0.7 log-plus-one_multiply_fusion
  339.8 0.0 all-gather.2.cloned.1.call-done
  339.8 0.0 copy-start
  339.8 18.2 %fusion = (f32[1024]{0:T(1024)S(1)}, f32[1024,1024]{1,0:T(8,128)S(1)}) fusion(f32[1024]{0:T(1024)S(1)} %all-reduce, f32[1024]{0:T(1024)S(1)} %log-plus-one_multiply_fusion, f32[1024,1024]{1,0:T(8,128)} %all-gather.2.cloned.1.call-done, f32[1024,1024]{1,0:T(8,128)} %param.6), kind=kOutput, calls=%fused_computation.1 | convolution fusion | flops 12888046592 | bytes 12595200 | tf_op jit(solution)/shard_map/dot_general | solution.py:9
  358.0 0.0 copy-done
  358.0 16.2 %fusion.1 = f32[1024,1024]{1,0:T(8,128)} fusion(f32[1024,1024]{1,0:T(8,128)S(1)} %copy-done, f32[1024,1024]{1,0:T(8,128)S(1)} %get-tuple-element.3, f32[1024]{0:T(1024)S(1)} %all-reduce, f32[1024]{0:T(1024)S(1)} %log-plus-one_multiply_fusion), kind=kOutput, calls=%fused_computation.2 | convolution fusion | flops 12886999040 | bytes 12591104 | tf_op jit(solution)/shard_map/dot_general | solution.py:13
  374.3 0.0 all-reduce.3.cloned.1.call-update
  374.3 4.4 psum.15
  378.7 113.3 %all-reduce.3.cloned.1.call-done = f32[1024,1024]{1,0:T(8,128)} async-done(((f32[1024,1024]{1,0:T(8,128)}), f32[1024,1024]{1,0:T(8,128)}) %all-reduce.3.cloned.1.call-update) | async-done | bytes 4194320 | tf_op jit(solution)/shard_map/psum | solution.py:29
  492.0 4.8 copy.8
  (1 shorter events, 0.0 us)
Async XLA Ops:
  7.2 332.6 %all-gather.2.cloned.1.call-start = ((), (), s32[]{:S(2)}) async-start(), calls=%async_computation | async-start | bytes 4227072 | tf_op jit(solution)/shard_map/all_gather | solution.py:25
  7.9 484.1 %all-reduce.3.cloned.1.call-start = ((), (), s32[]{:S(2)}) async-start(), calls=%async_computation.1 | async-start | bytes 8388608 | tf_op jit(solution)/shard_map/psum | solution.py:29
  339.8 18.3 %copy-start = (f32[1024,1024]{1,0:T(8,128)S(1)}, f32[1024,1024]{1,0:T(8,128)}, u32[]{:S(2)}) copy-start(f32[1024,1024]{1,0:T(8,128)} %all-gather.2.cloned.1.call-done) | copy-start | bytes 12582916
Sparse Core Ops, SparseCore 0:
  11.8 123.1 all-gather.1
  374.4 117.4 all-reduce.2
where the time goes:
time: 504 us
  blocking collectives  333 us (66%)
  waiting for transfers between devices  114 us (23%)
  matrix products  34.5 us (7%)
  between operations  14.7 us (3%)
  local copies, waits for them, and re-layouts  6.92 us (1%)
    unnamed x1, blocking collectives  328 us
    psum x1, waiting for transfers between devices, body(): numerator, weights = lax.psum((partial_num, partial_mass), 'grp')  113 us
    dot_general x1, matrix products, make_update(): jnp.dot(part_rows, shard.T, precision=lax.Precision.HIGHEST, preferred_el...  18.2 us
    dot_general x1, matrix products, make_update(): jnp.dot(resp.T, part_rows, precision=lax.Precision.HIGHEST, preferred_ele...  16.2 us
  transfers between devices with their start and end apart: 2, of which 1 were waited for; matrix products, arithmetic and copies ran while one was open for 1% of the time, Pallas kernels for 0%

commit v1 on v0

v1 whole, which is shorter than its diff:
```python
import functools

import jax
import jax.numpy as jnp
from jax import lax
from jax.experimental import pallas as pl
from jax.experimental.pallas import tpu as pltpu
from jax.sharding import Mesh, PartitionSpec as P

f32, bf16 = jnp.float32, jnp.bfloat16
AXES = ("x", "yh", "z", "core", "yl")
NT = (((1,), (1,)), ((), ()))
NN = (((1,), (0,)), ((), ()))
LANES = 128
VMEM = pl.BlockSpec(memory_space=pltpu.VMEM)


def flat(x, y, z, c):
    return ((x % 4 * 2 + y % 4 // 2) * 8 + z % 8) * 4 + c * 2 + y % 2


def pairs(target):
    return [
        (flat(x, y, z, c), flat(*target(x, y, z, c)))
        for x in range(4) for y in range(4) for z in range(8) for c in range(2)
    ]


LOOP = [(0, 0), (1, 0), (2, 0), (3, 0), (3, 1), (2, 1), (1, 1), (0, 1)]


def ring(step):
    def target(x, y, z, c):
        if c == 0:
            return x, y, z + step, c
        nx, ny = LOOP[(LOOP.index((x, y % 2)) + step) % 8]
        return nx, y // 2 * 2 + ny, z, c
    return pairs(target)


FORWARD, BACKWARD = ring(1), ring(-1)
SWAP = pairs(lambda x, y, z, c: (x, y, z, 1 - c))
FIRST = [[flat(x, y, z, 0) for x in range(4) for y in range(4)] for z in range(8)] + [
    [flat(x, 2 * yh + yl, z, 1) for z in range(8) for yh in range(2)] for x in range(4) for yl in range(2)
]


def halves(v):
    high = v.astype(bf16)
    return high, (v - high.astype(f32)).astype(bf16)


def dot(a, b, dims):
    return lax.dot_general(a, b, dims, preferred_element_type=f32)


def product(a_high, a_low, b_high, b_low, dims):
    return dot(a_high, b_high, dims) + dot(a_low, b_high, dims) + dot(a_high, b_low, dims)


def prepare_kernel(shard, counts, high, low, penalty):
    high[...], low[...] = halves(shard[...])
    pen = 0.5 * jnp.log(1.0 + counts[...].astype(f32))
    for i in range(8):
        penalty[pl.ds(i * LANES, LANES), :] = jnp.transpose(jnp.broadcast_to(pen[i : i + 1, :], (LANES, LANES)))


def prepare(shard, counts):
    k, d = shard.shape
    return pl.pallas_call(
        prepare_kernel,
        in_specs=[VMEM] * 2,
        out_specs=[VMEM] * 3,
        out_shape=[pltpu.VMEM((k, d), bf16), pltpu.VMEM((k, d), bf16), pltpu.VMEM((k, LANES), f32)],
        compiler_params=pltpu.CompilerParams(vmem_limit_bytes=8 * 2**20),
        cost_estimate=pl.CostEstimate(flops=4 * k * d, bytes_accessed=8 * k * d, transcendentals=0),
        name="prepare",
    )(in_vmem(shard), in_vmem(counts.reshape(8, LANES)))


def in_vmem(v):
    return pltpu.with_memory_space_constraint(v, pltpu.VMEM)


def load_rows(blocks, row_high, row_low):
    norms = []
    d = row_high.shape[1]
    for i, block in enumerate(blocks):
        n = block.shape[0]
        row_high[pl.ds(i * n, n), :], row_low[pl.ds(i * n, n), :] = halves(block[:, :d])
        norms.append(jnp.transpose(block[:, d:])[0:1, :])
    return jnp.concatenate(norms, axis=1)


def responses(high, low, penalty, norms, row_high, row_low, at):
    score = product(high[at, :], low[at, :], row_high[...], row_low[...], NT)
    resp = jnp.exp(score - penalty[at, 0:1] - norms)
    total = product(*halves(resp), row_high[...], row_low[...], NN)
    mass = sum(resp[:, i : i + LANES] for i in range(0, resp.shape[1], LANES))
    return total, mass


def chunk_kernel(count, fresh, step, *refs):
    blocks, refs = refs[:count], refs[count:]
    if fresh:
        high, low, penalty, total_out, mass_out, row_high, row_low = refs
    else:
        high, low, penalty, total_in, mass_in, total_out, mass_out, row_high, row_low = refs
    norms = load_rows(blocks, row_high, row_low)
    for start in range(0, high.shape[0], step):
        at = pl.ds(start, step)
        total, mass = responses(high, low, penalty, norms, row_high, row_low, at)
        if fresh:
            total_out[at, :], mass_out[at, :] = total, mass
        else:
            total_out[at, :], mass_out[at, :] = total_in[at, :] + total, mass_in[at, :] + mass


def cost(rows, k, d):
    return pl.CostEstimate(flops=12 * rows * k * d, bytes_accessed=4 * rows * d, transcendentals=rows * k)


def chunk(blocks, high, low, penalty, sums):
    k, d = high.shape
    count, rows = len(blocks), sum(b.shape[0] for b in blocks)
    args = [*blocks, high, low, penalty, *sums]
    return pl.pallas_call(
        functools.partial(chunk_kernel, count, not sums, 512),
        in_specs=[VMEM] * len(args),
        out_specs=[VMEM] * 2,
        out_shape=[pltpu.VMEM((k, d), f32), pltpu.VMEM((k, LANES), f32)],
        scratch_shapes=[pltpu.VMEM((rows, d), bf16)] * 2,
        input_output_aliases={count + 3: 0, count + 4: 1} if sums else {},
        compiler_params=pltpu.CompilerParams(vmem_limit_bytes=20 * 2**20),
        cost_estimate=cost(rows, k, d),
        name="chunk",
    )(*[in_vmem(a) for a in args])


def last_kernel(count, step, *refs):
    blocks, refs = refs[:count], refs[count:]
    high, low, penalty, total_in, mass_in, total_out, mass_out, row_high, row_low, norm_row = refs
    i = pl.program_id(0)

    @pl.when(i == 0)
    def _():
        norm_row[0:1, :] = load_rows(blocks, row_high, row_low)

    at = pl.ds(pl.multiple_of(i * step, step), step)
    total, mass = responses(high, low, penalty, norm_row[0:1, :], row_high, row_low, at)
    total_out[...] = total_in[at, :] + total
    mass = mass_in[at, :] + mass
    for j in range(step // LANES):
        part = jnp.transpose(mass[j * LANES : (j + 1) * LANES, :])
        mass_out[0, j : j + 1, :] = jnp.sum(part, axis=0, keepdims=True)


def last(blocks, high, low, penalty, sums):
    k, d = high.shape
    step = 256
    count, rows = len(blocks), sum(b.shape[0] for b in blocks)
    args = [*blocks, high, low, penalty, *sums]
    numerator, weights = pl.pallas_call(
        functools.partial(last_kernel, count, step),
        grid=(k // step,),
        in_specs=[VMEM] * len(args),
        out_specs=[
            pl.BlockSpec((step, d), lambda i: (i, 0)),
            pl.BlockSpec((1, step // LANES, LANES), lambda i: (i, 0, 0)),
        ],
        out_shape=[jax.ShapeDtypeStruct((k, d), f32), jax.ShapeDtypeStruct((k // step, step // LANES, LANES), f32)],
        scratch_shapes=[pltpu.VMEM((rows, d), bf16)] * 2 + [pltpu.VMEM((8, rows), f32)],
        compiler_params=pltpu.CompilerParams(vmem_limit_bytes=20 * 2**20),
        cost_estimate=cost(rows, k, d),
        name="last",
    )(*[in_vmem(a) for a in args])
    return numerator, weights.reshape(k)


def body(rows, lognorm, centroids, counts):
    def send(v, how):
        return lax.ppermute(v, AXES, how)

    n = rows.shape[0]
    own = jnp.concatenate([rows, jnp.broadcast_to(lognorm[:, None], (n, LANES))], axis=1)
    own = lax.all_to_all(
        jnp.broadcast_to(own, (16, *own.shape)), AXES, 0, 0, axis_index_groups=FIRST, tiled=True
    ).reshape(16 * n, -1)
    prepared = prepare(centroids, counts)
    up, down = send(own, FORWARD), send(own, BACKWARD)
    sums = chunk([own, send(own, SWAP)], *prepared, ())
    for _ in range(2):
        blocks = [up, down]
        up, down = send(up, FORWARD), send(down, BACKWARD)
        sums = chunk(blocks + [send(b, SWAP) for b in blocks], *prepared, sums)
    blocks = [up, down]
    up = send(up, FORWARD)
    sums = chunk(blocks + [send(b, SWAP) for b in blocks], *prepared, sums)
    return last([up, send(up, SWAP)], *prepared, sums)


def solution(mesh):
    split = Mesh(mesh.devices.reshape(4, 2, 8, 2, 2), AXES)
    blk = ("x", "yh", "z", "core")
    in_specs = (P(AXES, None), P(AXES), P(blk, None), P(blk))
    out_specs = (P(blk, None), P(blk))
    return jax.shard_map(body, mesh=split, in_specs=in_specs, out_specs=out_specs, check_vma=False)
```

time: 504 us -> 89.5 us (0.18)
  blocking collectives: 333 us -> 26.6 us
  waiting for transfers between devices: 114 us -> 8.39 us
  Pallas kernels: 0 us -> 37.8 us
  matrix products: 34.5 us -> 0 us
  between operations: 14.7 us -> 0.73 us
  starting transfers between devices: 0.08 us -> 11.3 us
    unnamed x1 -> x0, blocking collectives: 328 us -> none
    psum x1 -> x0, waiting for transfers between devices: 113 us -> none  [body(): numerator, weights = lax.psum((partial_num, partial_mass), 'grp')]
    pallas_call x0 -> x6, Pallas kernels: none -> 37.8 us  [the longest x4 27.7 us: chunk(): pl.pallas_call(functools.partial(chunk_kernel, count, not sums, 512), in_...]
    dot_general x2 -> x0, matrix products: 34.5 us -> none  [the longest x1 18.2 us: make_update(): jnp.dot(part_rows, shard.T, precision=lax.Precision.HIGHEST, preferred_el...]
    all_to_all x0 -> x1, blocking collectives: none -> 26.6 us  [body(): lax.all_to_all(jnp.broadcast_to(own, (16, *own.shape)), AXES, 0, 0, axis_...]
    ppermute x0 -> x15, starting transfers between devices: none -> 11.3 us  [send(): return lax.ppermute(v, AXES, how)]
    ppermute x0 -> x15, waiting for transfers between devices: none -> 8.39 us  [send(): return lax.ppermute(v, AXES, how)]
  transfers between devices with their start and end apart: 2 -> 15, of which waited for: 1 -> 3; matrix products, arithmetic and copies ran while one was open for 1% -> 0% of each run, Pallas kernels for 0% -> 33%
where the time goes in v1:
time: 89.5 us; the launch traced here: 89.2 us
  Pallas kernels  37.8 us (42%)
  blocking collectives  26.6 us (30%)
  starting transfers between devices  11.3 us (13%)
  waiting for transfers between devices  8.39 us (9%)
  local copies, waits for them, and re-layouts  3.64 us (4%)
    pallas_call x4, Pallas kernels, chunk(): pl.pallas_call(functools.partial(chunk_kernel, count, not sums, 512), in_...  27.7 us
    all_to_all x1, blocking collectives, body(): lax.all_to_all(jnp.broadcast_to(own, (16, *own.shape)), AXES, 0, 0, axis_...  26.6 us
    ppermute x15, starting transfers between devices, send(): return lax.ppermute(v, AXES, how)  11.3 us
    pallas_call x1, Pallas kernels, last(): pl.pallas_call(functools.partial(last_kernel, count, step), grid=(k // st...  8.81 us
    ppermute x15, waiting for transfers between devices, send(): return lax.ppermute(v, AXES, how)  8.39 us
    unnamed x4, local copies, waits for them, and re-layouts  2.87 us
  transfers between devices with their start and end apart: 15, of which 3 were waited for; matrix products, arithmetic and copies ran while one was open for 0% of the time, Pallas kernels for 33%

profile of v1, /device:TPU:1, one launch (start us, length us, event | category | flops | bytes accessed | tf_op | source)
XLA Modules:
  0.0 89.2 jit_solution(18046423767721752890)
XLA Ops:
  0.6 0.7 broadcast_in_dim.4
  1.4 0.8 pad_maximum_fusion
  2.2 26.6 %all_to_all.5 = f32[16,8,1152]{2,1,0:T(8,128)S(1)} all-to-all(f32[16,8,1152]{2,1,0:T(8,128)S(1)} %broadcast_in_dim.10), channel_id=1, replica_groups={{0,1,32,33,64,65,96,97,128,129,160,161,192,193,224,225},{4,5,36,37,68,6..., dimensions={0} | all-to-all | bytes 1179648 | tf_op jit(solution)/shard_map/all_to_all | solution.py:186
  28.7 1.3 %collective-permute-start = (f32[128,1152]{1,0:T(8,128)S(1)}, f32[128,1152]{1,0:T(8,128)S(1)}, u32[]{:S(2)}, u32[]{:S(2)}) collective-permute-start(f32[128,1152]{1,0:T(8,128)S(1)} %bitcast.3), channel_id=1, source_target_pairs={{0,4},{2,66},{4,8},{6,70},{8,12},{10,74},{12,16},{14,78},{16,20},{... | collective-permute-start | bytes 1769480 | tf_op jit(solution)/shard_map/ppermute | solution.py:182
  30.0 0.2 collective-permute-start.5
  30.2 7.3 %collective-permute-done.refs_0_ = f32[128,1152]{1,0:T(8,128)S(1)} collective-permute-done((f32[128,1152]{1,0:T(8,128)S(1)}, f32[128,1152]{1,0:T(8,128)S(1)}, u32[]{:S(2)}, u32[]{:S(2)}) %collective-permute-start) | collective-permute-done | bytes 589856 | tf_op jit(solution)/shard_map/ppermute | solution.py:182
  37.5 1.6 %collective-permute-start.1 = (f32[128,1152]{1,0:T(8,128)S(1)}, f32[128,1152]{1,0:T(8,128)S(1)}, u32[]{:S(2)}, u32[]{:S(2)}) collective-permute-start(f32[128,1152]{1,0:T(8,128)S(1)} %collective-permute-done.refs_0_), channel_id=1, source_target_pairs={{0,4},{2,66},{4,8},{6,70},{8,12},{10,74},{12,16},{14,78},{16,20},{... | collective-permute-start | bytes 1769480 | tf_op jit(solution)/shard_map/ppermute | solution.py:182
  39.1 0.2 collective-permute-start.6
  39.2 0.5 collective-permute-start.13
  39.7 2.2 %copy-done = f32[1024,1024]{1,0:T(8,128)S(1)} copy-done((f32[1024,1024]{1,0:T(8,128)S(1)}, f32[1024,1024]{1,0:T(8,128)}, u32[]{:S(2)}) %copy-start) | copy-done | bytes 4194328
  41.9 0.7 copy-done.1
  42.6 1.3 %prepare.1 = (bf16[1024,1024]{1,0:T(8,128)(2,1)S(1)}, bf16[1024,1024]{1,0:T(8,128)(2,1)S(1)}, f32[1024,128]{1,0:T(8,128)S(1)}) custom-call(f32[1024,1024]{1,0:T(8,128)S(1)} %copy-done, s32[8,128]{1,0:T(8,128)S(1)} %bitcast.7), custom_call_target="tpu_custom_call" | custom-call | flops 4194304 | bytes 8388608 | tf_op jit(solution)/shard_map/prepare/pallas_call | solution.py:70
  43.9 6.7 %chunk.4 = (f32[1024,1024]{1,0:T(8,128)S(1)}, f32[1024,128]{1,0:T(8,128)S(1)}) custom-call(f32[128,1152]{1,0:T(8,128)S(1)} %bitcast.6, f32[128,1152]{1,0:T(8,128)S(1)} %collective-permute-done.14.refs_1_, bf16[1024,1024]{1,0:T(8,128)(2,1)S(1)} %get-tuple-element.15.refs_2_.refs_4_, bf16[1024,1024]{1,0:T(8,128)(2,1)S(1)} %get-tuple-element.16.refs_3_.refs_5_, ...), custom_call_target="tpu_custom_call" | custom-call | flops 3221225472 | bytes 1048576 | tf_op jit(solution)/shard_map/chunk/pallas_call | solution.py:127
  50.7 1.4 %collective-permute-start.2 = (f32[128,1152]{1,0:T(8,128)S(1)}, f32[128,1152]{1,0:T(8,128)S(1)}, u32[]{:S(2)}, u32[]{:S(2)}) collective-permute-start(f32[128,1152]{1,0:T(8,128)S(1)} %collective-permute-done.1.refs_0_), channel_id=1, source_target_pairs={{0,4},{2,66},{4,8},{6,70},{8,12},{10,74},{12,16},{14,78},{16,20},{... | collective-permute-start | bytes 1769480 | tf_op jit(solution)/shard_map/ppermute | solution.py:182
  52.1 0.2 collective-permute-start.7
  52.3 7.0 %chunk.5 = (f32[1024,1024]{1,0:T(8,128)S(1)}, f32[1024,128]{1,0:T(8,128)S(1)}) custom-call(f32[128,1152]{1,0:T(8,128)S(1)} %collective-permute-done.refs_0_, f32[128,1152]{1,0:T(8,128)S(1)} %collective-permute-done.5.refs_1_, f32[128,1152]{1,0:T(8,128)S(1)} %collective-permute-done.12.refs_2_, ...), custom_call_target="tpu_custom_call", output_to_operand_aliasing={{0}: (7, {}), {1}: (8, {})} | custom-call | flops 6442450944 | bytes 2097152 | tf_op jit(solution)/shard_map/chunk/pallas_call | solution.py:127
  59.4 0.4 collective-permute-done.2.refs_0_
  59.8 2.5 %collective-permute-start.8 = (f32[128,1152]{1,0:T(8,128)S(1)}, f32[128,1152]{1,0:T(8,128)S(1)}, u32[]{:S(2)}, u32[]{:S(2)}) collective-permute-start(f32[128,1152]{1,0:T(8,128)S(1)} %collective-permute-done.2.refs_0_), channel_id=1, source_target_pairs={{0,2},{2,0},{4,6},{6,4},{8,10},{10,8},{12,14},{14,12},{16,18},{18,... | collective-permute-start | bytes 1769480 | tf_op jit(solution)/shard_map/ppermute | solution.py:182
  62.3 1.3 %collective-permute-start.3 = (f32[128,1152]{1,0:T(8,128)S(1)}, f32[128,1152]{1,0:T(8,128)S(1)}, u32[]{:S(2)}, u32[]{:S(2)}) collective-permute-start(f32[128,1152]{1,0:T(8,128)S(1)} %collective-permute-done.2.refs_0_), channel_id=1, source_target_pairs={{0,4},{2,66},{4,8},{6,70},{8,12},{10,74},{12,16},{14,78},{16,20},{... | collective-permute-start | bytes 1769480 | tf_op jit(solution)/shard_map/ppermute | solution.py:182
  63.6 7.0 %chunk.6 = (f32[1024,1024]{1,0:T(8,128)S(1)}, f32[1024,128]{1,0:T(8,128)S(1)}) custom-call(f32[128,1152]{1,0:T(8,128)S(1)} %collective-permute-done.1.refs_0_, f32[128,1152]{1,0:T(8,128)S(1)} %collective-permute-done.6.refs_1_, f32[128,1152]{1,0:T(8,128)S(1)} %collective-permute-done.10.refs_2_, ...), custom_call_target="tpu_custom_call", output_to_operand_aliasing={{0}: (7, {}), {1}: (8, {})} | custom-call | flops 6442450944 | bytes 2097152 | tf_op jit(solution)/shard_map/chunk/pallas_call | solution.py:127
  70.7 0.7 collective-permute-done.3.refs_0_
  71.3 2.1 %collective-permute-start.4 = (f32[128,1152]{1,0:T(8,128)S(1)}, f32[128,1152]{1,0:T(8,128)S(1)}, u32[]{:S(2)}, u32[]{:S(2)}) collective-permute-start(f32[128,1152]{1,0:T(8,128)S(1)} %collective-permute-done.3.refs_0_), channel_id=1, source_target_pairs={{0,2},{2,0},{4,6},{6,4},{8,10},{10,8},{12,14},{14,12},{16,18},{18,... | collective-permute-start | bytes 1769480 | tf_op jit(solution)/shard_map/ppermute | solution.py:182
  73.4 7.0 %chunk.7 = (f32[1024,1024]{1,0:T(8,128)S(1)}, f32[1024,128]{1,0:T(8,128)S(1)}) custom-call(f32[128,1152]{1,0:T(8,128)S(1)} %collective-permute-done.2.refs_0_, f32[128,1152]{1,0:T(8,128)S(1)} %collective-permute-done.7.refs_1_, f32[128,1152]{1,0:T(8,128)S(1)} %collective-permute-done.8.refs_2_, ...), custom_call_target="tpu_custom_call", output_to_operand_aliasing={{0}: (7, {}), {1}: (8, {})} | custom-call | flops 6442450944 | bytes 2097152 | tf_op jit(solution)/shard_map/chunk/pallas_call | solution.py:127
  80.4 8.8 %last.1 = (f32[1024,1024]{1,0:T(8,128)}, f32[4,2,128]{2,1,0:T(2,128)}) custom-call(f32[128,1152]{1,0:T(8,128)S(1)} %collective-permute-done.3.refs_0_, f32[128,1152]{1,0:T(8,128)S(1)} %collective-permute-done.4.refs_1_, bf16[1024,1024]{1,0:T(8,128)(2,1)S(1)} %get-tuple-element.15.refs_2_.refs_4_, bf16[1024,1024]{1,0:T(8,128)(2,1)S(1)} %get-tuple-element.16.refs_3_.refs_5_, ...), custom_call_target="tpu_custom_call" | custom-call | flops 3221225472 | bytes 1048576 | tf_op jit(solution)/shard_map/last/pallas_call | solution.py:163
  (20 shorter events, 0.2 us)
Async XLA Ops:
  28.7 8.7 %collective-permute-start = (f32[128,1152]{1,0:T(8,128)S(1)}, f32[128,1152]{1,0:T(8,128)S(1)}, u32[]{:S(2)}, u32[]{:S(2)}) collective-permute-start(f32[128,1152]{1,0:T(8,128)S(1)} %bitcast.3), channel_id=1, source_target_pairs={{0,4},{2,66},{4,8},{6,70},{8,12},{10,74},{12,16},{14,78},{16,20},{... | collective-permute-start | bytes 1769480 | tf_op jit(solution)/shard_map/ppermute | solution.py:182
  30.0 9.0 %collective-permute-start.5 = (f32[128,1152]{1,0:T(8,128)S(1)}, f32[128,1152]{1,0:T(8,128)S(1)}, u32[]{:S(2)}, u32[]{:S(2)}) collective-permute-start(f32[128,1152]{1,0:T(8,128)S(1)} %bitcast.4), channel_id=1, source_target_pairs={{0,28},{2,3},{4,0},{6,7},{8,4},{10,11},{12,8},{14,15},{16,12},{18,... | collective-permute-start | bytes 1769480 | tf_op jit(solution)/shard_map/ppermute | solution.py:182
  30.2 13.7 %collective-permute-start.14 = (f32[128,1152]{1,0:T(8,128)S(1)}, f32[128,1152]{1,0:T(8,128)S(1)}, u32[]{:S(2)}, u32[]{:S(2)}) collective-permute-start(f32[128,1152]{1,0:T(8,128)S(1)} %bitcast.5), channel_id=1, source_target_pairs={{0,2},{2,0},{4,6},{6,4},{8,10},{10,8},{12,14},{14,12},{16,18},{18,... | collective-permute-start | bytes 1769480 | tf_op jit(solution)/shard_map/ppermute | solution.py:182
  37.5 13.1 %collective-permute-start.1 = (f32[128,1152]{1,0:T(8,128)S(1)}, f32[128,1152]{1,0:T(8,128)S(1)}, u32[]{:S(2)}, u32[]{:S(2)}) collective-permute-start(f32[128,1152]{1,0:T(8,128)S(1)} %collective-permute-done.refs_0_), channel_id=1, source_target_pairs={{0,4},{2,66},{4,8},{6,70},{8,12},{10,74},{12,16},{14,78},{16,20},{... | collective-permute-start | bytes 1769480 | tf_op jit(solution)/shard_map/ppermute | solution.py:182
  39.1 13.0 %collective-permute-start.6 = (f32[128,1152]{1,0:T(8,128)S(1)}, f32[128,1152]{1,0:T(8,128)S(1)}, u32[]{:S(2)}, u32[]{:S(2)}) collective-permute-start(f32[128,1152]{1,0:T(8,128)S(1)} %collective-permute-done.5.refs_1_), channel_id=1, source_target_pairs={{0,28},{2,3},{4,0},{6,7},{8,4},{10,11},{12,8},{14,15},{16,12},{18,... | collective-permute-start | bytes 1769480 | tf_op jit(solution)/shard_map/ppermute | solution.py:182
  39.2 12.9 %collective-permute-start.12 = (f32[128,1152]{1,0:T(8,128)S(1)}, f32[128,1152]{1,0:T(8,128)S(1)}, u32[]{:S(2)}, u32[]{:S(2)}) collective-permute-start(f32[128,1152]{1,0:T(8,128)S(1)} %collective-permute-done.refs_0_), channel_id=1, source_target_pairs={{0,2},{2,0},{4,6},{6,4},{8,10},{10,8},{12,14},{14,12},{16,18},{18,... | collective-permute-start | bytes 1769480 | tf_op jit(solution)/shard_map/ppermute | solution.py:182
  39.2 13.1 %collective-permute-start.13 = (f32[128,1152]{1,0:T(8,128)S(1)}, f32[128,1152]{1,0:T(8,128)S(1)}, u32[]{:S(2)}, u32[]{:S(2)}) collective-permute-start(f32[128,1152]{1,0:T(8,128)S(1)} %collective-permute-done.5.refs_1_), channel_id=1, source_target_pairs={{0,2},{2,0},{4,6},{6,4},{8,10},{10,8},{12,14},{14,12},{16,18},{18,... | collective-permute-start | bytes 1769480 | tf_op jit(solution)/shard_map/ppermute | solution.py:182
  39.7 2.2 %copy-start = (f32[1024,1024]{1,0:T(8,128)S(1)}, f32[1024,1024]{1,0:T(8,128)}, u32[]{:S(2)}) copy-start(f32[1024,1024]{1,0:T(8,128)} %shard.1) | copy-start | bytes 12582916
  41.9 0.7 copy-start.1
  50.6 13.0 %collective-permute-start.10 = (f32[128,1152]{1,0:T(8,128)S(1)}, f32[128,1152]{1,0:T(8,128)S(1)}, u32[]{:S(2)}, u32[]{:S(2)}) collective-permute-start(f32[128,1152]{1,0:T(8,128)S(1)} %collective-permute-done.1.refs_0_), channel_id=1, source_target_pairs={{0,2},{2,0},{4,6},{6,4},{8,10},{10,8},{12,14},{14,12},{16,18},{18,... | collective-permute-start | bytes 1769480 | tf_op jit(solution)/shard_map/ppermute | solution.py:182
  50.7 9.1 %collective-permute-start.2 = (f32[128,1152]{1,0:T(8,128)S(1)}, f32[128,1152]{1,0:T(8,128)S(1)}, u32[]{:S(2)}, u32[]{:S(2)}) collective-permute-start(f32[128,1152]{1,0:T(8,128)S(1)} %collective-permute-done.1.refs_0_), channel_id=1, source_target_pairs={{0,4},{2,66},{4,8},{6,70},{8,12},{10,74},{12,16},{14,78},{16,20},{... | collective-permute-start | bytes 1769480 | tf_op jit(solution)/shard_map/ppermute | solution.py:182
  52.1 11.5 %collective-permute-start.11 = (f32[128,1152]{1,0:T(8,128)S(1)}, f32[128,1152]{1,0:T(8,128)S(1)}, u32[]{:S(2)}, u32[]{:S(2)}) collective-permute-start(f32[128,1152]{1,0:T(8,128)S(1)} %collective-permute-done.6.refs_1_), channel_id=1, source_target_pairs={{0,2},{2,0},{4,6},{6,4},{8,10},{10,8},{12,14},{14,12},{16,18},{18,... | collective-permute-start | bytes 1769480 | tf_op jit(solution)/shard_map/ppermute | solution.py:182
  52.1 11.5 %collective-permute-start.7 = (f32[128,1152]{1,0:T(8,128)S(1)}, f32[128,1152]{1,0:T(8,128)S(1)}, u32[]{:S(2)}, u32[]{:S(2)}) collective-permute-start(f32[128,1152]{1,0:T(8,128)S(1)} %collective-permute-done.6.refs_1_), channel_id=1, source_target_pairs={{0,28},{2,3},{4,0},{6,7},{8,4},{10,11},{12,8},{14,15},{16,12},{18,... | collective-permute-start | bytes 1769480 | tf_op jit(solution)/shard_map/ppermute | solution.py:182
  59.8 13.6 %collective-permute-start.8 = (f32[128,1152]{1,0:T(8,128)S(1)}, f32[128,1152]{1,0:T(8,128)S(1)}, u32[]{:S(2)}, u32[]{:S(2)}) collective-permute-start(f32[128,1152]{1,0:T(8,128)S(1)} %collective-permute-done.2.refs_0_), channel_id=1, source_target_pairs={{0,2},{2,0},{4,6},{6,4},{8,10},{10,8},{12,14},{14,12},{16,18},{18,... | collective-permute-start | bytes 1769480 | tf_op jit(solution)/shard_map/ppermute | solution.py:182
  62.3 9.0 %collective-permute-start.3 = (f32[128,1152]{1,0:T(8,128)S(1)}, f32[128,1152]{1,0:T(8,128)S(1)}, u32[]{:S(2)}, u32[]{:S(2)}) collective-permute-start(f32[128,1152]{1,0:T(8,128)S(1)} %collective-permute-done.2.refs_0_), channel_id=1, source_target_pairs={{0,4},{2,66},{4,8},{6,70},{8,12},{10,74},{12,16},{14,78},{16,20},{... | collective-permute-start | bytes 1769480 | tf_op jit(solution)/shard_map/ppermute | solution.py:182
  63.6 9.8 %collective-permute-start.9 = (f32[128,1152]{1,0:T(8,128)S(1)}, f32[128,1152]{1,0:T(8,128)S(1)}, u32[]{:S(2)}, u32[]{:S(2)}) collective-permute-start(f32[128,1152]{1,0:T(8,128)S(1)} %collective-permute-done.7.refs_1_), channel_id=1, source_target_pairs={{0,2},{2,0},{4,6},{6,4},{8,10},{10,8},{12,14},{14,12},{16,18},{18,... | collective-permute-start | bytes 1769480 | tf_op jit(solution)/shard_map/ppermute | solution.py:182
  71.3 9.1 %collective-permute-start.4 = (f32[128,1152]{1,0:T(8,128)S(1)}, f32[128,1152]{1,0:T(8,128)S(1)}, u32[]{:S(2)}, u32[]{:S(2)}) collective-permute-start(f32[128,1152]{1,0:T(8,128)S(1)} %collective-permute-done.3.refs_0_), channel_id=1, source_target_pairs={{0,2},{2,0},{4,6},{6,4},{8,10},{10,8},{12,14},{14,12},{16,18},{18,... | collective-permute-start | bytes 1769480 | tf_op jit(solution)/shard_map/ppermute | solution.py:182

commit v2 on v1

v2 whole, which is shorter than its diff:
```python
import functools

import jax
import jax.numpy as jnp
from jax import lax
from jax.experimental import pallas as pl
from jax.experimental.pallas import tpu as pltpu
from jax.sharding import Mesh, PartitionSpec as P

f32, bf16 = jnp.float32, jnp.bfloat16
AXES = ("x", "yh", "z", "core", "yl")
NT = (((1,), (1,)), ((), ()))
NN = (((1,), (0,)), ((), ()))
LANES = 128
VMEM = pl.BlockSpec(memory_space=pltpu.VMEM)


def flat(x, y, z, c):
    return ((x % 4 * 2 + y % 4 // 2) * 8 + z % 8) * 4 + c * 2 + y % 2


def pairs(target):
    return [
        (flat(x, y, z, c), flat(*target(x, y, z, c)))
        for x in range(4) for y in range(4) for z in range(8) for c in range(2)
    ]


LOOP = [(0, 0), (1, 0), (2, 0), (3, 0), (3, 1), (2, 1), (1, 1), (0, 1)]


def ring(step):
    def target(x, y, z, c):
        if c == 0:
            return x, y, z + step, c
        yh, yl = y // 2, y % 2
        nx, nh = LOOP[(LOOP.index(((x + 2 * yl) % 4, yh)) + step) % 8]
        return nx + 2 * yl, nh * 2 + yl, z, c
    return pairs(target)


FORWARD, BACKWARD = ring(1), ring(-1)
SWAP = pairs(lambda x, y, z, c: (x, y, z, 1 - c))
FIRST = [[flat(x, y, z, 0) for x in range(4) for y in range(4)] for z in range(8)] + [
    [flat(x, 2 * yh + yl, z, 1) for z in range(8) for yl in range(2)] for x in range(4) for yh in range(2)
]


def halves(v):
    high = v.astype(bf16)
    return high, (v - high.astype(f32)).astype(bf16)


def dot(a, b, dims):
    return lax.dot_general(a, b, dims, preferred_element_type=f32)


def product(a_high, a_low, b_high, b_low, dims):
    return dot(a_high, b_high, dims) + dot(a_low, b_high, dims) + dot(a_high, b_low, dims)


def prepare_kernel(parts, shard, counts, high, low, penalty, landed, sems):
    n = shard.shape[0] // parts
    places = [pl.ds(i * n, n) for i in range(parts)]
    copies = [pltpu.make_async_copy(shard.at[at, :], landed.at[at, :], sems.at[i]) for i, at in enumerate(places)]
    for copy in copies:
        copy.start()
    pen = 0.5 * jnp.log(1.0 + counts[...].astype(f32))
    for i in range(pen.shape[0]):
        penalty[pl.ds(i * LANES, LANES), :] = jnp.transpose(jnp.broadcast_to(pen[i : i + 1, :], (LANES, LANES)))
    for copy, at in zip(copies, places):
        copy.wait()
        high[at, :], low[at, :] = halves(landed[at, :])


def prepare(shard, counts):
    k, d = shard.shape
    parts = 8
    return pl.pallas_call(
        functools.partial(prepare_kernel, parts),
        in_specs=[pl.BlockSpec(memory_space=pl.ANY), VMEM],
        out_specs=[VMEM] * 3,
        out_shape=[pltpu.VMEM((k, d), bf16), pltpu.VMEM((k, d), bf16), pltpu.VMEM((k, LANES), f32)],
        scratch_shapes=[pltpu.VMEM((k, d), f32), pltpu.SemaphoreType.DMA((parts,))],
        compiler_params=pltpu.CompilerParams(vmem_limit_bytes=8 * 2**20),
        cost_estimate=pl.CostEstimate(flops=4 * k * d, bytes_accessed=8 * k * d, transcendentals=0),
        name="prepare",
    )(pltpu.with_memory_space_constraint(shard, pltpu.HBM), counts.reshape(k // LANES, LANES))


def pack_kernel(rows, norms, packed):
    n, d = rows.shape
    diagonal = lax.broadcasted_iota(jnp.int32, (n, n), 0) == lax.broadcasted_iota(jnp.int32, (n, n), 1)
    norm = jnp.sum(jnp.where(diagonal, norms[...], 0.0), axis=1, keepdims=True)
    packed[:, :, :d] = jnp.broadcast_to(rows[...][None], (packed.shape[0], n, d))
    packed[:, :, d:] = jnp.broadcast_to(norm[None], (packed.shape[0], n, LANES))


def pack(rows, lognorm, copies):
    n, d = rows.shape
    return pl.pallas_call(
        pack_kernel,
        in_specs=[VMEM] * 2,
        out_specs=VMEM,
        out_shape=pltpu.VMEM((copies, n, d + LANES), f32),
        name="pack",
    )(rows, lognorm.reshape(1, n))


MARGIN = 8


def join_kernel(parts, joined):
    count, n, width = parts.shape
    half, d = count // 2 * n, joined.shape[1]
    for i in range(count):
        joined[pl.ds(i * n + (i >= count // 2) * MARGIN, n), :] = parts[i, :, :d]
    norms = jnp.transpose(parts[:, :, d:].reshape(count * n, LANES))[:MARGIN, :]
    joined[pl.ds(half, MARGIN), :] = jnp.concatenate([norms, jnp.zeros((MARGIN, d - count * n), f32)], axis=1)


def join(parts):
    count, n, width = parts.shape
    return pl.pallas_call(
        join_kernel,
        in_specs=[VMEM],
        out_specs=VMEM,
        out_shape=pltpu.VMEM((count * n + MARGIN, width - LANES), f32),
        name="join",
    )(in_vmem(parts))


def in_vmem(v):
    return pltpu.with_memory_space_constraint(v, pltpu.VMEM)


def load_rows(blocks, row_high, row_low):
    norms, row = [], 0
    for kind, block in blocks:
        n = block.shape[0] - MARGIN
        middle = {"whole": n // 2, "front": n, "back": 0}[kind]
        first = n if kind == "back" else 0
        norms.append(block[middle : middle + 1, first : first + n])
        for start, end in ((0, middle), (middle + MARGIN, n + MARGIN)):
            if start < end:
                at = pl.ds(row, end - start)
                row_high[at, :], row_low[at, :] = halves(block[start:end, :])
                row += end - start
    return jnp.concatenate(norms, axis=1)


def rows_in(blocks):
    return sum(b.shape[0] - MARGIN for b in blocks)


def respond(high, low, penalty, norms, row_high, row_low, resp_high, resp_low, at):
    score = product(high[at, :], low[at, :], row_high[...], row_low[...], NT)
    resp = jnp.exp(score - penalty[at, 0:1] - norms)
    resp_high[at, :], resp_low[at, :] = halves(resp)
    return sum(resp[:, i : i + LANES] for i in range(0, resp.shape[1], LANES))


def gather_up(row_high, row_low, resp_high, resp_low, at):
    return product(resp_high[at, :], resp_low[at, :], row_high[...], row_low[...], NN)


def chunk_kernel(kinds, fresh, step, *refs):
    count = len(kinds)
    blocks, refs = list(zip(kinds, refs[:count])), refs[count:]
    if fresh:
        high, low, penalty, total_out, mass_out, *work = refs
    else:
        high, low, penalty, total_in, mass_in, total_out, mass_out, *work = refs
    norms = load_rows(blocks, *work[:2])
    places = [pl.ds(start, step) for start in range(0, high.shape[0], step)]
    for at in places:
        mass = respond(high, low, penalty, norms, *work, at)
        mass_out[at, :] = mass if fresh else mass_in[at, :] + mass
    for at in places:
        total = gather_up(*work, at)
        total_out[at, :] = total if fresh else total_in[at, :] + total


def scratch(rows, k, d):
    return [pltpu.VMEM((rows, d), bf16)] * 2 + [pltpu.VMEM((k, rows), bf16)] * 2


def cost(rows, k, d):
    return pl.CostEstimate(flops=12 * rows * k * d, bytes_accessed=4 * rows * d, transcendentals=rows * k)


def chunk(blocks, high, low, penalty, sums):
    k, d = high.shape
    count, rows = len(blocks), rows_in(blocks)
    args = [*blocks, high, low, penalty, *sums]
    return pl.pallas_call(
        functools.partial(chunk_kernel, ["whole"] * count, not sums, 512),
        in_specs=[VMEM] * len(args),
        out_specs=[VMEM] * 2,
        out_shape=[pltpu.VMEM((k, d), f32), pltpu.VMEM((k, LANES), f32)],
        scratch_shapes=scratch(rows, k, d),
        input_output_aliases={count + 3: 0, count + 4: 1} if sums else {},
        compiler_params=pltpu.CompilerParams(vmem_limit_bytes=20 * 2**20),
        cost_estimate=cost(rows, k, d),
        name="chunk",
    )(*[in_vmem(a) for a in args])


def last_kernel(kinds, step, out_step, *refs):
    count = len(kinds)
    blocks, refs = list(zip(kinds, refs[:count])), refs[count:]
    high, low, penalty, total_in, mass_in, total_out, mass_out, done, sems, *work = refs
    norms = load_rows(blocks, *work[:2])
    k = high.shape[0]
    for start in range(0, k, step):
        at = pl.ds(start, step)
        mass = mass_in[at, :] + respond(high, low, penalty, norms, *work, at)
        for j in range(step // LANES):
            part = jnp.transpose(mass[j * LANES : (j + 1) * LANES, :])
            mass_out[pl.ds(start // LANES + j, 1), :] = jnp.sum(part, axis=0, keepdims=True)
    copies = []
    for i, start in enumerate(range(0, k, out_step)):
        at = pl.ds(start, out_step)
        done[at, :] = total_in[at, :] + gather_up(*work, at)
        copies.append(pltpu.make_async_copy(done.at[at, :], total_out.at[at, :], sems.at[i]))
        copies[-1].start()
    for copy in copies:
        copy.wait()


def last(blocks, high, low, penalty, sums):
    k, d = high.shape
    step, out_step = 512, 128
    count, rows = len(blocks), rows_in(blocks)
    args = [*blocks, high, low, penalty, *sums]
    numerator, weights = pl.pallas_call(
        functools.partial(last_kernel, ["front", "back"] * (count // 2), step, out_step),
        in_specs=[VMEM] * len(args),
        out_specs=[pl.BlockSpec(memory_space=pl.ANY), VMEM],
        out_shape=[jax.ShapeDtypeStruct((k, d), f32), jax.ShapeDtypeStruct((k // LANES, LANES), f32)],
        scratch_shapes=[pltpu.VMEM((k, d), f32), pltpu.SemaphoreType.DMA((k // out_step,))] + scratch(rows, k, d),
        compiler_params=pltpu.CompilerParams(vmem_limit_bytes=20 * 2**20),
        cost_estimate=cost(rows, k, d),
        name="last",
    )(*[in_vmem(a) for a in args])
    return numerator, weights.reshape(k)


def after(v, other):
    return lax.optimization_barrier((v, other))[0]


def body(rows, lognorm, centroids, counts):
    def send(v, how):
        return lax.ppermute(v, AXES, how)

    own = lax.all_to_all(pack(rows, lognorm, 16), AXES, 0, 0, axis_index_groups=FIRST, tiled=True)
    own = join(own)
    prepared = prepare(centroids, counts)
    up, down = send(own, FORWARD), send(own, BACKWARD)
    sums = chunk([own, send(own, SWAP)], *prepared, ())
    for _ in range(2):
        up, down, sums = after(up, sums), after(down, sums), after(sums, (up, down))
        blocks = [after(up, down), after(down, up)]
        up, down = send(up, FORWARD), send(down, BACKWARD)
        sums = chunk(blocks + [send(b, SWAP) for b in blocks], *prepared, sums)
    up, down, sums = after(up, sums), after(down, sums), after(sums, (up, down))
    half = rows_in([up]) // 2
    far = [send(up[: half + MARGIN], FORWARD), send(down[half:], BACKWARD)]
    up, down = after(up, down), after(down, up)
    swapped = [send(up, SWAP), send(down, SWAP)]
    sums = chunk([up, down], *prepared, sums)
    far, sums = after(far, sums), after(sums, far)
    far_swapped = [send(b, SWAP) for b in far]
    sums = chunk(swapped, *prepared, sums)
    return last(far + far_swapped, *prepared, sums)


def solution(mesh):
    split = Mesh(mesh.devices.reshape(4, 2, 8, 2, 2), AXES)
    blk = ("x", "yh", "z", "core")
    in_specs = (P(AXES, None), P(AXES), P(blk, None), P(blk))
    out_specs = (P(blk, None), P(blk))
    return jax.shard_map(body, mesh=split, in_specs=in_specs, out_specs=out_specs, check_vma=False)
```

time: 89.5 us -> 78.8 us (0.88)
  Pallas kernels: 37.8 us -> 33.7 us
  blocking collectives: 26.6 us -> 23.4 us
  local copies, waits for them, and re-layouts: 3.64 us -> 0.73 us
  waiting for transfers between devices: 8.39 us -> 10.5 us
  starting transfers between devices: 11.3 us -> 9.28 us
    pallas_call x6 -> x9, Pallas kernels: 37.8 us -> 33.7 us  [the longest x5 25.5 us: chunk(): pl.pallas_call(functools.partial(chunk_kernel, ['whole'] * count, not sum...]
    all_to_all x1, blocking collectives: 26.6 us -> 23.4 us  [body(): lax.all_to_all(pack(rows, lognorm, 16), AXES, 0, 0, axis_index_groups=FIR...]
    unnamed x4 -> x2, local copies, waits for them, and re-layouts: 2.87 us -> 0.69 us
    ppermute x15 -> x17, waiting for transfers between devices: 8.39 us -> 10.5 us  [send(): return lax.ppermute(v, AXES, how)]
    ppermute x15 -> x17, starting transfers between devices: 11.3 us -> 9.28 us  [send(): return lax.ppermute(v, AXES, how)]
  transfers between devices with their start and end apart: 15 -> 17, of which waited for: 3 -> 7; matrix products, arithmetic and copies ran while one was open for 0% -> 0% of each run, Pallas kernels for 33% -> 35%
where the time goes in v2:
time: 78.8 us; the launch traced here: 78.5 us
  Pallas kernels  33.7 us (43%)
  blocking collectives  23.4 us (30%)
  waiting for transfers between devices  10.5 us (13%)
  starting transfers between devices  9.28 us (12%)
  between operations  0.94 us (1%)
    pallas_call x5, Pallas kernels, chunk(): pl.pallas_call(functools.partial(chunk_kernel, ['whole'] * count, not sum...  25.5 us
    all_to_all x1, blocking collectives, body(): lax.all_to_all(pack(rows, lognorm, 16), AXES, 0, 0, axis_index_groups=FIR...  23.4 us
    ppermute x17, waiting for transfers between devices, send(): return lax.ppermute(v, AXES, how)  10.5 us
    ppermute x17, starting transfers between devices, send(): return lax.ppermute(v, AXES, how)  9.28 us
    pallas_call x1, Pallas kernels, last(): pl.pallas_call(functools.partial(last_kernel, ['front', 'back'] * (count...  5 us
    pallas_call x1, Pallas kernels, prepare(): pl.pallas_call(functools.partial(prepare_kernel, parts), in_specs=[pl.Blo...  2.31 us
  transfers between devices with their start and end apart: 17, of which 7 were waited for; matrix products, arithmetic and copies ran while one was open for 0% of the time, Pallas kernels for 35%

profile of v2, /device:TPU:1, one launch (start us, length us, event | category | flops | bytes accessed | tf_op | source)
XLA Modules:
  0.0 78.5 jit_solution(8129857946449608269)
XLA Ops:
  0.6 0.8 %pack.1 = f32[16,8,1152]{2,1,0:T(8,128)S(1)} custom-call(f32[8,1024]{1,0:T(8,128)} %rows.1, f32[1,8]{1,0:T(1,128)} %bitcast.4), custom_call_target="tpu_custom_call" | custom-call | tf_op jit(solution)/shard_map/pack/pallas_call | solution.py:101
  1.5 23.4 %all_to_all.5.parts = f32[16,8,1152]{2,1,0:T(8,128)S(1)} all-to-all(f32[16,8,1152]{2,1,0:T(8,128)S(1)} %pack.1), channel_id=1, replica_groups={{0,1,32,33,64,65,96,97,128,129,160,161,192,193,224,225},{4,5,36,37,68,6..., dimensions={0} | all-to-all | bytes 1179648 | tf_op jit(solution)/shard_map/all_to_all | solution.py:257
  25.1 2.7 %collective-permute-start.3 = (f32[136,1024]{1,0:T(8,128)S(1)}, f32[136,1024]{1,0:T(8,128)S(1)}, u32[]{:S(2)}, u32[]{:S(2)}) collective-permute-start(f32[136,1024]{1,0:T(8,128)S(1)} %join.1.refs_0_), channel_id=1, source_target_pairs={{0,28},{2,34},{4,0},{6,38},{8,4},{10,42},{12,8},{14,46},{16,12},{1... | collective-permute-start | bytes 1671176 | tf_op jit(solution)/shard_map/ppermute | solution.py:255
  27.8 0.7 copy-done
  28.4 2.3 %prepare.1 = (bf16[1024,1024]{1,0:T(8,128)(2,1)S(1)}, bf16[1024,1024]{1,0:T(8,128)(2,1)S(1)}, f32[1024,128]{1,0:T(8,128)S(1)}) custom-call(f32[1024,1024]{1,0:T(8,128)} %shard.1, s32[8,128]{1,0:T(8,128)S(1)} %bitcast.3), custom_call_target="tpu_custom_call" | custom-call | flops 4194304 | bytes 8388608 | tf_op jit(solution)/shard_map/prepare/pallas_call | solution.py:79
  30.8 3.5 %chunk.5 = (f32[1024,1024]{1,0:T(8,128)S(1)}, f32[1024,128]{1,0:T(8,128)S(1)}) custom-call(f32[136,1024]{1,0:T(8,128)S(1)} %join.1.refs_0_, f32[136,1024]{1,0:T(8,128)S(1)} %collective-permute-done.1.refs_1_, bf16[1024,1024]{1,0:T(8,128)(2,1)S(1)} %get-tuple-element.39.refs_2_.refs_4_, bf16[1024,1024]{1,0:T(8,128)(2,1)S(1)} %get-tuple-element.40.refs_3_.refs_5_, ...), custom_call_target="tpu_custom_call" | custom-call | flops 3221225472 | bytes 1048576 | tf_op jit(solution)/shard_map/chunk/pallas_call | solution.py:196
  34.3 3.3 %collective-permute-done.refs_0_ = f32[136,1024]{1,0:T(8,128)S(1)} collective-permute-done((f32[136,1024]{1,0:T(8,128)S(1)}, f32[136,1024]{1,0:T(8,128)S(1)}, u32[]{:S(2)}, u32[]{:S(2)}) %collective-permute-start) | collective-permute-done | bytes 557088 | tf_op jit(solution)/shard_map/ppermute | solution.py:255
  37.6 0.5 collective-permute-start.4
  38.2 1.2 %collective-permute-start.7 = (f32[136,1024]{1,0:T(8,128)S(1)}, f32[136,1024]{1,0:T(8,128)S(1)}, u32[]{:S(2)}, u32[]{:S(2)}) collective-permute-start(f32[136,1024]{1,0:T(8,128)S(1)} %collective-permute-done.3.refs_1_), channel_id=1, source_target_pairs={{0,28},{2,34},{4,0},{6,38},{8,4},{10,42},{12,8},{14,46},{16,12},{1... | collective-permute-start | bytes 1671176 | tf_op jit(solution)/shard_map/ppermute | solution.py:255
  39.6 0.8 collective-permute-done.4.refs_2_
  40.4 7.2 %chunk.6 = (f32[1024,1024]{1,0:T(8,128)S(1)}, f32[1024,128]{1,0:T(8,128)S(1)}) custom-call(f32[136,1024]{1,0:T(8,128)S(1)} %collective-permute-done.refs_0_, f32[136,1024]{1,0:T(8,128)S(1)} %collective-permute-done.3.refs_1_, f32[136,1024]{1,0:T(8,128)S(1)} %collective-permute-done.4.refs_2_, ...), custom_call_target="tpu_custom_call", output_to_operand_aliasing={{0}: (7, {}), {1}: (8, {})} | custom-call | flops 6442450944 | bytes 2097152 | tf_op jit(solution)/shard_map/chunk/pallas_call | solution.py:196
  47.6 1.6 %collective-permute-done.2.refs_0_ = f32[136,1024]{1,0:T(8,128)S(1)} collective-permute-done((f32[136,1024]{1,0:T(8,128)S(1)}, f32[136,1024]{1,0:T(8,128)S(1)}, u32[]{:S(2)}, u32[]{:S(2)}) %collective-permute-start.2) | collective-permute-done | bytes 557088 | tf_op jit(solution)/shard_map/ppermute | solution.py:255
  49.7 0.9 %collective-permute-start.11 = (f32[136,1024]{1,0:T(8,128)S(1)}, f32[136,1024]{1,0:T(8,128)S(1)}, u32[]{:S(2)}, u32[]{:S(2)}) collective-permute-start(f32[136,1024]{1,0:T(8,128)S(1)} %collective-permute-done.7.refs_1_), channel_id=1, source_target_pairs={{0,28},{2,34},{4,0},{6,38},{8,4},{10,42},{12,8},{14,46},{16,12},{1... | collective-permute-start | bytes 1671176 | tf_op jit(solution)/shard_map/ppermute | solution.py:255
  50.6 0.6 collective-permute-start.6
  51.2 0.8 collective-permute-done.8.refs_2_
  52.0 7.2 %chunk.7 = (f32[1024,1024]{1,0:T(8,128)S(1)}, f32[1024,128]{1,0:T(8,128)S(1)}) custom-call(f32[136,1024]{1,0:T(8,128)S(1)} %collective-permute-done.2.refs_0_, f32[136,1024]{1,0:T(8,128)S(1)} %collective-permute-done.7.refs_1_, f32[136,1024]{1,0:T(8,128)S(1)} %collective-permute-done.8.refs_2_, ...), custom_call_target="tpu_custom_call", output_to_operand_aliasing={{0}: (7, {}), {1}: (8, {})} | custom-call | flops 6442450944 | bytes 2097152 | tf_op jit(solution)/shard_map/chunk/pallas_call | solution.py:196
  59.1 1.3 %collective-permute-done.6.refs_0_ = f32[136,1024]{1,0:T(8,128)S(1)} collective-permute-done((f32[136,1024]{1,0:T(8,128)S(1)}, f32[136,1024]{1,0:T(8,128)S(1)}, u32[]{:S(2)}, u32[]{:S(2)}) %collective-permute-start.6) | collective-permute-done | bytes 557088 | tf_op jit(solution)/shard_map/ppermute | solution.py:255
  61.0 0.9 %collective-permute-start.12 = (f32[72,1024]{1,0:T(8,128)S(1)}, f32[72,1024]{1,0:T(8,128)S(1)}, u32[]{:S(2)}, u32[]{:S(2)}) collective-permute-start(f32[72,1024]{1,0:T(8,128)S(1)} %slice.7), channel_id=1, source_target_pairs={{0,28},{2,34},{4,0},{6,38},{8,4},{10,42},{12,8},{14,46},{16,12},{1... | collective-permute-start | bytes 884744 | tf_op jit(solution)/shard_map/ppermute | solution.py:255
  62.0 0.6 collective-permute-start.10
  62.6 3.8 %chunk.8 = (f32[1024,1024]{1,0:T(8,128)S(1)}, f32[1024,128]{1,0:T(8,128)S(1)}) custom-call(f32[136,1024]{1,0:T(8,128)S(1)} %collective-permute-done.6.refs_0_, f32[136,1024]{1,0:T(8,128)S(1)} %collective-permute-done.11.refs_1_, bf16[1024,1024]{1,0:T(8,128)(2,1)S(1)} %get-tuple-element.39.refs_2_.refs_4_, ...), custom_call_target="tpu_custom_call", output_to_operand_aliasing={{0}: (5, {}), {1}: (6, {})} | custom-call | flops 3221225472 | bytes 1048576 | tf_op jit(solution)/shard_map/chunk/pallas_call | solution.py:196
  66.4 0.6 collective-permute-done.12.refs_1_
  67.0 2.1 %collective-permute-done.10.refs_0_ = f32[72,1024]{1,0:T(8,128)S(1)} collective-permute-done((f32[72,1024]{1,0:T(8,128)S(1)}, f32[72,1024]{1,0:T(8,128)S(1)}, u32[]{:S(2)}, u32[]{:S(2)}) %collective-permute-start.10) | collective-permute-done | bytes 294944 | tf_op jit(solution)/shard_map/ppermute | solution.py:255
  69.6 3.8 %chunk.9 = (f32[1024,1024]{1,0:T(8,128)S(1)}, f32[1024,128]{1,0:T(8,128)S(1)}) custom-call(f32[136,1024]{1,0:T(8,128)S(1)} %collective-permute-done.15.refs_0_, f32[136,1024]{1,0:T(8,128)S(1)} %collective-permute-done.16.refs_1_, bf16[1024,1024]{1,0:T(8,128)(2,1)S(1)} %get-tuple-element.39.refs_2_.refs_4_, ...), custom_call_target="tpu_custom_call", output_to_operand_aliasing={{0}: (5, {}), {1}: (6, {})} | custom-call | flops 3221225472 | bytes 1048576 | tf_op jit(solution)/shard_map/chunk/pallas_call | solution.py:196
  73.4 5.0 %last.1 = (f32[1024,1024]{1,0:T(8,128)}, f32[8,128]{1,0:T(8,128)}) custom-call(f32[72,1024]{1,0:T(8,128)S(1)} %collective-permute-done.10.refs_0_, f32[72,1024]{1,0:T(8,128)S(1)} %collective-permute-done.12.refs_1_, f32[72,1024]{1,0:T(8,128)S(1)} %collective-permute-done.13.refs_2_, f32[72,1024]{1,0:T(8,128)S(1)} %collective-permute-done.14.refs_3_, ...), custom_call_target="tpu_custom_call" | custom-call | flops 3221225472 | bytes 1048576 | tf_op jit(solution)/shard_map/last/pallas_call | solution.py:236
  (24 shorter events, 2.1 us)
Async XLA Ops:
  25.0 5.8 %collective-permute-start.1 = (f32[136,1024]{1,0:T(8,128)S(1)}, f32[136,1024]{1,0:T(8,128)S(1)}, u32[]{:S(2)}, u32[]{:S(2)}) collective-permute-start(f32[136,1024]{1,0:T(8,128)S(1)} %join.1.refs_0_), channel_id=1, source_target_pairs={{0,2},{2,0},{4,6},{6,4},{8,10},{10,8},{12,14},{14,12},{16,18},{18,... | collective-permute-start | bytes 1671176 | tf_op jit(solution)/shard_map/ppermute | solution.py:255
  25.1 9.3 %collective-permute-start.3 = (f32[136,1024]{1,0:T(8,128)S(1)}, f32[136,1024]{1,0:T(8,128)S(1)}, u32[]{:S(2)}, u32[]{:S(2)}) collective-permute-start(f32[136,1024]{1,0:T(8,128)S(1)} %join.1.refs_0_), channel_id=1, source_target_pairs={{0,28},{2,34},{4,0},{6,38},{8,4},{10,42},{12,8},{14,46},{16,12},{1... | collective-permute-start | bytes 1671176 | tf_op jit(solution)/shard_map/ppermute | solution.py:255
  27.8 9.9 %collective-permute-start = (f32[136,1024]{1,0:T(8,128)S(1)}, f32[136,1024]{1,0:T(8,128)S(1)}, u32[]{:S(2)}, u32[]{:S(2)}) collective-permute-start(f32[136,1024]{1,0:T(8,128)S(1)} %join.1.refs_0_), channel_id=1, source_target_pairs={{0,4},{2,66},{4,8},{6,70},{8,12},{10,74},{12,16},{14,78},{16,20},{... | collective-permute-start | bytes 1671176 | tf_op jit(solution)/shard_map/ppermute | solution.py:255
  27.8 0.7 copy-start
  37.6 2.0 %collective-permute-start.5 = (f32[136,1024]{1,0:T(8,128)S(1)}, f32[136,1024]{1,0:T(8,128)S(1)}, u32[]{:S(2)}, u32[]{:S(2)}) collective-permute-start(f32[136,1024]{1,0:T(8,128)S(1)} %collective-permute-done.3.refs_1_), channel_id=1, source_target_pairs={{0,2},{2,0},{4,6},{6,4},{8,10},{10,8},{12,14},{14,12},{16,18},{18,... | collective-permute-start | bytes 1671176 | tf_op jit(solution)/shard_map/ppermute | solution.py:255
  37.6 2.8 %collective-permute-start.4 = (f32[136,1024]{1,0:T(8,128)S(1)}, f32[136,1024]{1,0:T(8,128)S(1)}, u32[]{:S(2)}, u32[]{:S(2)}) collective-permute-start(f32[136,1024]{1,0:T(8,128)S(1)} %collective-permute-done.refs_0_), channel_id=1, source_target_pairs={{0,2},{2,0},{4,6},{6,4},{8,10},{10,8},{12,14},{14,12},{16,18},{18,... | collective-permute-start | bytes 1671176 | tf_op jit(solution)/shard_map/ppermute | solution.py:255
  38.2 9.4 %collective-permute-start.7 = (f32[136,1024]{1,0:T(8,128)S(1)}, f32[136,1024]{1,0:T(8,128)S(1)}, u32[]{:S(2)}, u32[]{:S(2)}) collective-permute-start(f32[136,1024]{1,0:T(8,128)S(1)} %collective-permute-done.3.refs_1_), channel_id=1, source_target_pairs={{0,28},{2,34},{4,0},{6,38},{8,4},{10,42},{12,8},{14,46},{16,12},{1... | collective-permute-start | bytes 1671176 | tf_op jit(solution)/shard_map/ppermute | solution.py:255
  39.3 9.9 %collective-permute-start.2 = (f32[136,1024]{1,0:T(8,128)S(1)}, f32[136,1024]{1,0:T(8,128)S(1)}, u32[]{:S(2)}, u32[]{:S(2)}) collective-permute-start(f32[136,1024]{1,0:T(8,128)S(1)} %collective-permute-done.refs_0_), channel_id=1, source_target_pairs={{0,4},{2,66},{4,8},{6,70},{8,12},{10,74},{12,16},{14,78},{16,20},{... | collective-permute-start | bytes 1671176 | tf_op jit(solution)/shard_map/ppermute | solution.py:255
  49.2 2.0 %collective-permute-start.9 = (f32[136,1024]{1,0:T(8,128)S(1)}, f32[136,1024]{1,0:T(8,128)S(1)}, u32[]{:S(2)}, u32[]{:S(2)}) collective-permute-start(f32[136,1024]{1,0:T(8,128)S(1)} %collective-permute-done.7.refs_1_), channel_id=1, source_target_pairs={{0,2},{2,0},{4,6},{6,4},{8,10},{10,8},{12,14},{14,12},{16,18},{18,... | collective-permute-start | bytes 1671176 | tf_op jit(solution)/shard_map/ppermute | solution.py:255
  49.3 2.7 %collective-permute-start.8 = (f32[136,1024]{1,0:T(8,128)S(1)}, f32[136,1024]{1,0:T(8,128)S(1)}, u32[]{:S(2)}, u32[]{:S(2)}) collective-permute-start(f32[136,1024]{1,0:T(8,128)S(1)} %collective-permute-done.2.refs_0_), channel_id=1, source_target_pairs={{0,2},{2,0},{4,6},{6,4},{8,10},{10,8},{12,14},{14,12},{16,18},{18,... | collective-permute-start | bytes 1671176 | tf_op jit(solution)/shard_map/ppermute | solution.py:255
  49.7 9.4 %collective-permute-start.11 = (f32[136,1024]{1,0:T(8,128)S(1)}, f32[136,1024]{1,0:T(8,128)S(1)}, u32[]{:S(2)}, u32[]{:S(2)}) collective-permute-start(f32[136,1024]{1,0:T(8,128)S(1)} %collective-permute-done.7.refs_1_), channel_id=1, source_target_pairs={{0,28},{2,34},{4,0},{6,38},{8,4},{10,42},{12,8},{14,46},{16,12},{1... | collective-permute-start | bytes 1671176 | tf_op jit(solution)/shard_map/ppermute | solution.py:255
  50.6 9.9 %collective-permute-start.6 = (f32[136,1024]{1,0:T(8,128)S(1)}, f32[136,1024]{1,0:T(8,128)S(1)}, u32[]{:S(2)}, u32[]{:S(2)}) collective-permute-start(f32[136,1024]{1,0:T(8,128)S(1)} %collective-permute-done.2.refs_0_), channel_id=1, source_target_pairs={{0,4},{2,66},{4,8},{6,70},{8,12},{10,74},{12,16},{14,78},{16,20},{... | collective-permute-start | bytes 1671176 | tf_op jit(solution)/shard_map/ppermute | solution.py:255
  60.5 9.1 %collective-permute-start.16 = (f32[136,1024]{1,0:T(8,128)S(1)}, f32[136,1024]{1,0:T(8,128)S(1)}, u32[]{:S(2)}, u32[]{:S(2)}) collective-permute-start(f32[136,1024]{1,0:T(8,128)S(1)} %collective-permute-done.11.refs_1_), channel_id=1, source_target_pairs={{0,2},{2,0},{4,6},{6,4},{8,10},{10,8},{12,14},{14,12},{16,18},{18,... | collective-permute-start | bytes 1671176 | tf_op jit(solution)/shard_map/ppermute | solution.py:255
  60.5 9.0 %collective-permute-start.15 = (f32[136,1024]{1,0:T(8,128)S(1)}, f32[136,1024]{1,0:T(8,128)S(1)}, u32[]{:S(2)}, u32[]{:S(2)}) collective-permute-start(f32[136,1024]{1,0:T(8,128)S(1)} %collective-permute-done.6.refs_0_), channel_id=1, source_target_pairs={{0,2},{2,0},{4,6},{6,4},{8,10},{10,8},{12,14},{14,12},{16,18},{18,... | collective-permute-start | bytes 1671176 | tf_op jit(solution)/shard_map/ppermute | solution.py:255
  61.0 5.9 %collective-permute-start.12 = (f32[72,1024]{1,0:T(8,128)S(1)}, f32[72,1024]{1,0:T(8,128)S(1)}, u32[]{:S(2)}, u32[]{:S(2)}) collective-permute-start(f32[72,1024]{1,0:T(8,128)S(1)} %slice.7), channel_id=1, source_target_pairs={{0,28},{2,34},{4,0},{6,38},{8,4},{10,42},{12,8},{14,46},{16,12},{1... | collective-permute-start | bytes 884744 | tf_op jit(solution)/shard_map/ppermute | solution.py:255
  62.0 7.1 %collective-permute-start.10 = (f32[72,1024]{1,0:T(8,128)S(1)}, f32[72,1024]{1,0:T(8,128)S(1)}, u32[]{:S(2)}, u32[]{:S(2)}) collective-permute-start(f32[72,1024]{1,0:T(8,128)S(1)} %slice.6), channel_id=1, source_target_pairs={{0,4},{2,66},{4,8},{6,70},{8,12},{10,74},{12,16},{14,78},{16,20},{... | collective-permute-start | bytes 884744 | tf_op jit(solution)/shard_map/ppermute | solution.py:255
  69.0 4.3 %collective-permute-start.13 = (f32[72,1024]{1,0:T(8,128)S(1)}, f32[72,1024]{1,0:T(8,128)S(1)}, u32[]{:S(2)}, u32[]{:S(2)}) collective-permute-start(f32[72,1024]{1,0:T(8,128)S(1)} %collective-permute-done.10.refs_0_), channel_id=1, source_target_pairs={{0,2},{2,0},{4,6},{6,4},{8,10},{10,8},{12,14},{14,12},{16,18},{18,... | collective-permute-start | bytes 884744 | tf_op jit(solution)/shard_map/ppermute | solution.py:255
  69.2 4.1 %collective-permute-start.14 = (f32[72,1024]{1,0:T(8,128)S(1)}, f32[72,1024]{1,0:T(8,128)S(1)}, u32[]{:S(2)}, u32[]{:S(2)}) collective-permute-start(f32[72,1024]{1,0:T(8,128)S(1)} %collective-permute-done.12.refs_1_), channel_id=1, source_target_pairs={{0,2},{2,0},{4,6},{6,4},{8,10},{10,8},{12,14},{14,12},{16,18},{18,... | collective-permute-start | bytes 884744 | tf_op jit(solution)/shard_map/ppermute | solution.py:255

commit v3 on v2

--- a/solution.py
+++ b/solution.py
@@ -112,11 +112,10 @@
 
 def join_kernel(parts, joined):
     count, n, width = parts.shape
-    half, d = count // 2 * n, joined.shape[1]
-    for i in range(count):
-        joined[pl.ds(i * n + (i >= count // 2) * MARGIN, n), :] = parts[i, :, :d]
-    norms = jnp.transpose(parts[:, :, d:].reshape(count * n, LANES))[:MARGIN, :]
-    joined[pl.ds(half, MARGIN), :] = jnp.concatenate([norms, jnp.zeros((MARGIN, d - count * n), f32)], axis=1)
+    rows, d = count * n, joined.shape[1]
+    joined[pl.ds(0, rows), :] = parts[:, :, :d].reshape(rows, d)
+    norms = jnp.transpose(parts[:, :, d:].reshape(rows, LANES))[:MARGIN, :]
+    joined[pl.ds(rows, MARGIN), :] = jnp.concatenate([norms, jnp.zeros((MARGIN, d - rows), f32)], axis=1)
 
 
 def join(parts):
@@ -135,17 +134,12 @@
 
 
 def load_rows(blocks, row_high, row_low):
-    norms, row = [], 0
-    for kind, block in blocks:
+    norms = []
+    for i, block in enumerate(blocks):
         n = block.shape[0] - MARGIN
-        middle = {"whole": n // 2, "front": n, "back": 0}[kind]
-        first = n if kind == "back" else 0
-        norms.append(block[middle : middle + 1, first : first + n])
-        for start, end in ((0, middle), (middle + MARGIN, n + MARGIN)):
-            if start < end:
-                at = pl.ds(row, end - start)
-                row_high[at, :], row_low[at, :] = halves(block[start:end, :])
-                row += end - start
+        at = pl.ds(i * n, n)
+        row_high[at, :], row_low[at, :] = halves(block[:n, :])
+        norms.append(block[n : n + 1, :n])
     return jnp.concatenate(norms, axis=1)
 
 
@@ -164,9 +158,8 @@
     return product(resp_high[at, :], resp_low[at, :], row_high[...], row_low[...], NN)
 
 
-def chunk_kernel(kinds, fresh, step, *refs):
-    count = len(kinds)
-    blocks, refs = list(zip(kinds, refs[:count])), refs[count:]
+def chunk_kernel(count, fresh, step, *refs):
+    blocks, refs = refs[:count], refs[count:]
     if fresh:
         high, low, penalty, total_out, mass_out, *work = refs
     else:
@@ -194,7 +187,7 @@
     count, rows = len(blocks), rows_in(blocks)
     args = [*blocks, high, low, penalty, *sums]
     return pl.pallas_call(
-        functools.partial(chunk_kernel, ["whole"] * count, not sums, 512),
+        functools.partial(chunk_kernel, count, not sums, 512),
         in_specs=[VMEM] * len(args),
         out_specs=[VMEM] * 2,
         out_shape=[pltpu.VMEM((k, d), f32), pltpu.VMEM((k, LANES), f32)],
@@ -206,9 +199,8 @@
     )(*[in_vmem(a) for a in args])
 
 
-def last_kernel(kinds, step, out_step, *refs):
-    count = len(kinds)
-    blocks, refs = list(zip(kinds, refs[:count])), refs[count:]
+def last_kernel(count, step, out_step, *refs):
+    blocks, refs = refs[:count], refs[count:]
     high, low, penalty, total_in, mass_in, total_out, mass_out, done, sems, *work = refs
     norms = load_rows(blocks, *work[:2])
     k = high.shape[0]
@@ -234,7 +226,7 @@
     count, rows = len(blocks), rows_in(blocks)
     args = [*blocks, high, low, penalty, *sums]
     numerator, weights = pl.pallas_call(
-        functools.partial(last_kernel, ["front", "back"] * (count // 2), step, out_step),
+        functools.partial(last_kernel, count, step, out_step),
         in_specs=[VMEM] * len(args),
         out_specs=[pl.BlockSpec(memory_space=pl.ANY), VMEM],
         out_shape=[jax.ShapeDtypeStruct((k, d), f32), jax.ShapeDtypeStruct((k // LANES, LANES), f32)],
@@ -265,15 +257,13 @@
         up, down = send(up, FORWARD), send(down, BACKWARD)
         sums = chunk(blocks + [send(b, SWAP) for b in blocks], *prepared, sums)
     up, down, sums = after(up, sums), after(down, sums), after(sums, (up, down))
-    half = rows_in([up]) // 2
-    far = [send(up[: half + MARGIN], FORWARD), send(down[half:], BACKWARD)]
+    far = send(down, BACKWARD)
     up, down = after(up, down), after(down, up)
     swapped = [send(up, SWAP), send(down, SWAP)]
     sums = chunk([up, down], *prepared, sums)
+    sums = chunk(swapped, *prepared, sums)
     far, sums = after(far, sums), after(sums, far)
-    far_swapped = [send(b, SWAP) for b in far]
-    sums = chunk(swapped, *prepared, sums)
-    return last(far + far_swapped, *prepared, sums)
+    return last([far, send(far, SWAP)], *prepared, sums)
 
 
 def solution(mesh):

time: 78.8 us -> 77.8 us (0.987)
  waiting for transfers between devices: 10.5 us -> 1.98 us
  starting transfers between devices: 9.28 us -> 16.3 us
    ppermute x17 -> x15, waiting for transfers between devices: 10.5 us -> 1.98 us  [send(): return lax.ppermute(v, AXES, how)]
    ppermute x17 -> x15, starting transfers between devices: 9.28 us -> 16.3 us  [send(): return lax.ppermute(v, AXES, how)]
  transfers between devices with their start and end apart: 17 -> 15, of which waited for: 7 -> 2; matrix products, arithmetic and copies ran while one was open for 0% -> 0% of each run, Pallas kernels for 35% -> 36%
where the time goes in v3:
time: 77.8 us; the launch traced here: 77 us
  Pallas kernels  33.7 us (43%)
  blocking collectives  23.4 us (30%)
  starting transfers between devices  16.3 us (21%)
  waiting for transfers between devices  1.98 us (3%)
  between operations  0.94 us (1%)
    pallas_call x5, Pallas kernels, chunk(): pl.pallas_call(functools.partial(chunk_kernel, count, not sums, 512), in_...  25.5 us
    all_to_all x1, blocking collectives, body(): lax.all_to_all(pack(rows, lognorm, 16), AXES, 0, 0, axis_index_groups=FIR...  23.4 us
    ppermute x15, starting transfers between devices, send(): return lax.ppermute(v, AXES, how)  16.3 us
    pallas_call x1, Pallas kernels, last(): pl.pallas_call(functools.partial(last_kernel, count, step, out_step), in_...  4.99 us
    pallas_call x1, Pallas kernels, prepare(): pl.pallas_call(functools.partial(prepare_kernel, parts), in_specs=[pl.Blo...  2.31 us
    ppermute x15, waiting for transfers between devices, send(): return lax.ppermute(v, AXES, how)  1.98 us
  transfers between devices with their start and end apart: 15, of which 2 were waited for; matrix products, arithmetic and copies ran while one was open for 0% of the time, Pallas kernels for 36%

profile of v3, /device:TPU:1, one launch (start us, length us, event | category | flops | bytes accessed | tf_op | source)
XLA Modules:
  0.0 77.0 jit_solution(9122096234094596354)
XLA Ops:
  0.6 0.8 %pack.1 = f32[16,8,1152]{2,1,0:T(8,128)S(1)} custom-call(f32[8,1024]{1,0:T(8,128)} %rows.1, f32[1,8]{1,0:T(1,128)} %bitcast.4), custom_call_target="tpu_custom_call" | custom-call | tf_op jit(solution)/shard_map/pack/pallas_call | solution.py:101
  1.5 23.4 %all_to_all.5.parts = f32[16,8,1152]{2,1,0:T(8,128)S(1)} all-to-all(f32[16,8,1152]{2,1,0:T(8,128)S(1)} %pack.1), channel_id=1, replica_groups={{0,1,32,33,64,65,96,97,128,129,160,161,192,193,224,225},{4,5,36,37,68,6..., dimensions={0} | all-to-all | bytes 1179648 | tf_op jit(solution)/shard_map/all_to_all | solution.py:249
  24.9 0.1 join.1.refs_0_
  25.1 1.3 %collective-permute-start.3 = (f32[136,1024]{1,0:T(8,128)S(1)}, f32[136,1024]{1,0:T(8,128)S(1)}, u32[]{:S(2)}, u32[]{:S(2)}) collective-permute-start(f32[136,1024]{1,0:T(8,128)S(1)} %join.1.refs_0_), channel_id=1, source_target_pairs={{0,4},{2,66},{4,8},{6,70},{8,12},{10,74},{12,16},{14,78},{16,20},{... | collective-permute-start | bytes 1671176 | tf_op jit(solution)/shard_map/ppermute | solution.py:247
  26.3 1.8 %collective-permute-start = (f32[136,1024]{1,0:T(8,128)S(1)}, f32[136,1024]{1,0:T(8,128)S(1)}, u32[]{:S(2)}, u32[]{:S(2)}) collective-permute-start(f32[136,1024]{1,0:T(8,128)S(1)} %join.1.refs_0_), channel_id=1, source_target_pairs={{0,28},{2,34},{4,0},{6,38},{8,4},{10,42},{12,8},{14,46},{16,12},{1... | collective-permute-start | bytes 1671176 | tf_op jit(solution)/shard_map/ppermute | solution.py:247
  28.1 0.7 copy-done
  28.8 2.3 %prepare.1 = (bf16[1024,1024]{1,0:T(8,128)(2,1)S(1)}, bf16[1024,1024]{1,0:T(8,128)(2,1)S(1)}, f32[1024,128]{1,0:T(8,128)S(1)}) custom-call(f32[1024,1024]{1,0:T(8,128)} %shard.1, s32[8,128]{1,0:T(8,128)S(1)} %bitcast.3), custom_call_target="tpu_custom_call" | custom-call | flops 4194304 | bytes 8388608 | tf_op jit(solution)/shard_map/prepare/pallas_call | solution.py:79
  31.1 3.5 %chunk.5 = (f32[1024,1024]{1,0:T(8,128)S(1)}, f32[1024,128]{1,0:T(8,128)S(1)}) custom-call(f32[136,1024]{1,0:T(8,128)S(1)} %join.1.refs_0_, f32[136,1024]{1,0:T(8,128)S(1)} %collective-permute-done.1.refs_1_, bf16[1024,1024]{1,0:T(8,128)(2,1)S(1)} %get-tuple-element.38.refs_2_.refs_4_, bf16[1024,1024]{1,0:T(8,128)(2,1)S(1)} %get-tuple-element.39.refs_3_.refs_5_, ...), custom_call_target="tpu_custom_call" | custom-call | flops 3221225472 | bytes 1048576 | tf_op jit(solution)/shard_map/chunk/pallas_call | solution.py:189
  34.7 0.4 collective-permute-done.3.refs_0_
  35.0 1.3 %collective-permute-start.5 = (f32[136,1024]{1,0:T(8,128)S(1)}, f32[136,1024]{1,0:T(8,128)S(1)}, u32[]{:S(2)}, u32[]{:S(2)}) collective-permute-start(f32[136,1024]{1,0:T(8,128)S(1)} %collective-permute-done.refs_1_), channel_id=1, source_target_pairs={{0,2},{2,0},{4,6},{6,4},{8,10},{10,8},{12,14},{14,12},{16,18},{18,... | collective-permute-start | bytes 1671176 | tf_op jit(solution)/shard_map/ppermute | solution.py:247
  36.3 1.2 %collective-permute-start.7 = (f32[136,1024]{1,0:T(8,128)S(1)}, f32[136,1024]{1,0:T(8,128)S(1)}, u32[]{:S(2)}, u32[]{:S(2)}) collective-permute-start(f32[136,1024]{1,0:T(8,128)S(1)} %collective-permute-done.3.refs_0_), channel_id=1, source_target_pairs={{0,4},{2,66},{4,8},{6,70},{8,12},{10,74},{12,16},{14,78},{16,20},{... | collective-permute-start | bytes 1671176 | tf_op jit(solution)/shard_map/ppermute | solution.py:247
  37.5 1.8 %collective-permute-start.2 = (f32[136,1024]{1,0:T(8,128)S(1)}, f32[136,1024]{1,0:T(8,128)S(1)}, u32[]{:S(2)}, u32[]{:S(2)}) collective-permute-start(f32[136,1024]{1,0:T(8,128)S(1)} %collective-permute-done.refs_1_), channel_id=1, source_target_pairs={{0,28},{2,34},{4,0},{6,38},{8,4},{10,42},{12,8},{14,46},{16,12},{1... | collective-permute-start | bytes 1671176 | tf_op jit(solution)/shard_map/ppermute | solution.py:247
  39.3 7.2 %chunk.6 = (f32[1024,1024]{1,0:T(8,128)S(1)}, f32[1024,128]{1,0:T(8,128)S(1)}) custom-call(f32[136,1024]{1,0:T(8,128)S(1)} %collective-permute-done.3.refs_0_, f32[136,1024]{1,0:T(8,128)S(1)} %collective-permute-done.refs_1_, f32[136,1024]{1,0:T(8,128)S(1)} %collective-permute-done.4.refs_2_, ...), custom_call_target="tpu_custom_call", output_to_operand_aliasing={{0}: (7, {}), {1}: (8, {})} | custom-call | flops 6442450944 | bytes 2097152 | tf_op jit(solution)/shard_map/chunk/pallas_call | solution.py:189
  46.5 1.1 %collective-permute-start.9 = (f32[136,1024]{1,0:T(8,128)S(1)}, f32[136,1024]{1,0:T(8,128)S(1)}, u32[]{:S(2)}, u32[]{:S(2)}) collective-permute-start(f32[136,1024]{1,0:T(8,128)S(1)} %collective-permute-done.2.refs_1_), channel_id=1, source_target_pairs={{0,2},{2,0},{4,6},{6,4},{8,10},{10,8},{12,14},{14,12},{16,18},{18,... | collective-permute-start | bytes 1671176 | tf_op jit(solution)/shard_map/ppermute | solution.py:247
  47.6 1.4 %collective-permute-start.11 = (f32[136,1024]{1,0:T(8,128)S(1)}, f32[136,1024]{1,0:T(8,128)S(1)}, u32[]{:S(2)}, u32[]{:S(2)}) collective-permute-start(f32[136,1024]{1,0:T(8,128)S(1)} %collective-permute-done.7.refs_0_), channel_id=1, source_target_pairs={{0,4},{2,66},{4,8},{6,70},{8,12},{10,74},{12,16},{14,78},{16,20},{... | collective-permute-start | bytes 1671176 | tf_op jit(solution)/shard_map/ppermute | solution.py:247
  48.9 1.6 %collective-permute-start.6 = (f32[136,1024]{1,0:T(8,128)S(1)}, f32[136,1024]{1,0:T(8,128)S(1)}, u32[]{:S(2)}, u32[]{:S(2)}) collective-permute-start(f32[136,1024]{1,0:T(8,128)S(1)} %collective-permute-done.2.refs_1_), channel_id=1, source_target_pairs={{0,28},{2,34},{4,0},{6,38},{8,4},{10,42},{12,8},{14,46},{16,12},{1... | collective-permute-start | bytes 1671176 | tf_op jit(solution)/shard_map/ppermute | solution.py:247
  50.5 7.2 %chunk.7 = (f32[1024,1024]{1,0:T(8,128)S(1)}, f32[1024,128]{1,0:T(8,128)S(1)}) custom-call(f32[136,1024]{1,0:T(8,128)S(1)} %collective-permute-done.7.refs_0_, f32[136,1024]{1,0:T(8,128)S(1)} %collective-permute-done.2.refs_1_, f32[136,1024]{1,0:T(8,128)S(1)} %collective-permute-done.8.refs_2_, ...), custom_call_target="tpu_custom_call", output_to_operand_aliasing={{0}: (7, {}), {1}: (8, {})} | custom-call | flops 6442450944 | bytes 2097152 | tf_op jit(solution)/shard_map/chunk/pallas_call | solution.py:189
  57.8 1.8 %collective-permute-start.13 = (f32[136,1024]{1,0:T(8,128)S(1)}, f32[136,1024]{1,0:T(8,128)S(1)}, u32[]{:S(2)}, u32[]{:S(2)}) collective-permute-start(f32[136,1024]{1,0:T(8,128)S(1)} %collective-permute-done.6.refs_1_), channel_id=1, source_target_pairs={{0,2},{2,0},{4,6},{6,4},{8,10},{10,8},{12,14},{14,12},{16,18},{18,... | collective-permute-start | bytes 1671176 | tf_op jit(solution)/shard_map/ppermute | solution.py:247
  59.5 2.0 %collective-permute-start.10 = (f32[136,1024]{1,0:T(8,128)S(1)}, f32[136,1024]{1,0:T(8,128)S(1)}, u32[]{:S(2)}, u32[]{:S(2)}) collective-permute-start(f32[136,1024]{1,0:T(8,128)S(1)} %collective-permute-done.6.refs_1_), channel_id=1, source_target_pairs={{0,28},{2,34},{4,0},{6,38},{8,4},{10,42},{12,8},{14,46},{16,12},{1... | collective-permute-start | bytes 1671176 | tf_op jit(solution)/shard_map/ppermute | solution.py:247
  61.5 3.8 %chunk.8 = (f32[1024,1024]{1,0:T(8,128)S(1)}, f32[1024,128]{1,0:T(8,128)S(1)}) custom-call(f32[136,1024]{1,0:T(8,128)S(1)} %collective-permute-done.11.refs_0_, f32[136,1024]{1,0:T(8,128)S(1)} %collective-permute-done.6.refs_1_, bf16[1024,1024]{1,0:T(8,128)(2,1)S(1)} %get-tuple-element.38.refs_2_.refs_4_, ...), custom_call_target="tpu_custom_call", output_to_operand_aliasing={{0}: (5, {}), {1}: (6, {})} | custom-call | flops 3221225472 | bytes 1048576 | tf_op jit(solution)/shard_map/chunk/pallas_call | solution.py:189
  65.4 3.8 %chunk.9 = (f32[1024,1024]{1,0:T(8,128)S(1)}, f32[1024,128]{1,0:T(8,128)S(1)}) custom-call(f32[136,1024]{1,0:T(8,128)S(1)} %collective-permute-done.12.refs_0_, f32[136,1024]{1,0:T(8,128)S(1)} %collective-permute-done.13.refs_1_, bf16[1024,1024]{1,0:T(8,128)(2,1)S(1)} %get-tuple-element.38.refs_2_.refs_4_, ...), custom_call_target="tpu_custom_call", output_to_operand_aliasing={{0}: (5, {}), {1}: (6, {})} | custom-call | flops 3221225472 | bytes 1048576 | tf_op jit(solution)/shard_map/chunk/pallas_call | solution.py:189
  69.2 1.1 %collective-permute-start.14 = (f32[136,1024]{1,0:T(8,128)S(1)}, f32[136,1024]{1,0:T(8,128)S(1)}, u32[]{:S(2)}, u32[]{:S(2)}) collective-permute-start(f32[136,1024]{1,0:T(8,128)S(1)} %collective-permute-done.10.refs_0_), channel_id=1, source_target_pairs={{0,2},{2,0},{4,6},{6,4},{8,10},{10,8},{12,14},{14,12},{16,18},{18,... | collective-permute-start | bytes 1671176 | tf_op jit(solution)/shard_map/ppermute | solution.py:247
  70.2 1.6 %collective-permute-done.14.refs_1_ = f32[136,1024]{1,0:T(8,128)S(1)} collective-permute-done((f32[136,1024]{1,0:T(8,128)S(1)}, f32[136,1024]{1,0:T(8,128)S(1)}, u32[]{:S(2)}, u32[]{:S(2)}) %collective-permute-start.14) | collective-permute-done | bytes 557088 | tf_op jit(solution)/shard_map/ppermute | solution.py:247
  71.8 5.0 %last.1 = (f32[1024,1024]{1,0:T(8,128)}, f32[8,128]{1,0:T(8,128)}) custom-call(f32[136,1024]{1,0:T(8,128)S(1)} %collective-permute-done.10.refs_0_, f32[136,1024]{1,0:T(8,128)S(1)} %collective-permute-done.14.refs_1_, bf16[1024,1024]{1,0:T(8,128)(2,1)S(1)} %get-tuple-element.38.refs_2_.refs_4_, bf16[1024,1024]{1,0:T(8,128)(2,1)S(1)} %get-tuple-element.39.refs_3_.refs_5_, ...), custom_call_target="tpu_custom_call" | custom-call | flops 3221225472 | bytes 1048576 | tf_op jit(solution)/shard_map/last/pallas_call | solution.py:228
  (18 shorter events, 0.1 us)
Async XLA Ops:
  25.0 6.1 %collective-permute-start.1 = (f32[136,1024]{1,0:T(8,128)S(1)}, f32[136,1024]{1,0:T(8,128)S(1)}, u32[]{:S(2)}, u32[]{:S(2)}) collective-permute-start(f32[136,1024]{1,0:T(8,128)S(1)} %join.1.refs_0_), channel_id=1, source_target_pairs={{0,2},{2,0},{4,6},{6,4},{8,10},{10,8},{12,14},{14,12},{16,18},{18,... | collective-permute-start | bytes 1671176 | tf_op jit(solution)/shard_map/ppermute | solution.py:247
  25.1 10.0 %collective-permute-start.3 = (f32[136,1024]{1,0:T(8,128)S(1)}, f32[136,1024]{1,0:T(8,128)S(1)}, u32[]{:S(2)}, u32[]{:S(2)}) collective-permute-start(f32[136,1024]{1,0:T(8,128)S(1)} %join.1.refs_0_), channel_id=1, source_target_pairs={{0,4},{2,66},{4,8},{6,70},{8,12},{10,74},{12,16},{14,78},{16,20},{... | collective-permute-start | bytes 1671176 | tf_op jit(solution)/shard_map/ppermute | solution.py:247
  26.3 8.7 %collective-permute-start = (f32[136,1024]{1,0:T(8,128)S(1)}, f32[136,1024]{1,0:T(8,128)S(1)}, u32[]{:S(2)}, u32[]{:S(2)}) collective-permute-start(f32[136,1024]{1,0:T(8,128)S(1)} %join.1.refs_0_), channel_id=1, source_target_pairs={{0,28},{2,34},{4,0},{6,38},{8,4},{10,42},{12,8},{14,46},{16,12},{1... | collective-permute-start | bytes 1671176 | tf_op jit(solution)/shard_map/ppermute | solution.py:247
  28.1 0.7 copy-start
  35.0 4.3 %collective-permute-start.5 = (f32[136,1024]{1,0:T(8,128)S(1)}, f32[136,1024]{1,0:T(8,128)S(1)}, u32[]{:S(2)}, u32[]{:S(2)}) collective-permute-start(f32[136,1024]{1,0:T(8,128)S(1)} %collective-permute-done.refs_1_), channel_id=1, source_target_pairs={{0,2},{2,0},{4,6},{6,4},{8,10},{10,8},{12,14},{14,12},{16,18},{18,... | collective-permute-start | bytes 1671176 | tf_op jit(solution)/shard_map/ppermute | solution.py:247
  36.3 3.0 %collective-permute-start.4 = (f32[136,1024]{1,0:T(8,128)S(1)}, f32[136,1024]{1,0:T(8,128)S(1)}, u32[]{:S(2)}, u32[]{:S(2)}) collective-permute-start(f32[136,1024]{1,0:T(8,128)S(1)} %collective-permute-done.3.refs_0_), channel_id=1, source_target_pairs={{0,2},{2,0},{4,6},{6,4},{8,10},{10,8},{12,14},{14,12},{16,18},{18,... | collective-permute-start | bytes 1671176 | tf_op jit(solution)/shard_map/ppermute | solution.py:247
  36.3 10.2 %collective-permute-start.7 = (f32[136,1024]{1,0:T(8,128)S(1)}, f32[136,1024]{1,0:T(8,128)S(1)}, u32[]{:S(2)}, u32[]{:S(2)}) collective-permute-start(f32[136,1024]{1,0:T(8,128)S(1)} %collective-permute-done.3.refs_0_), channel_id=1, source_target_pairs={{0,4},{2,66},{4,8},{6,70},{8,12},{10,74},{12,16},{14,78},{16,20},{... | collective-permute-start | bytes 1671176 | tf_op jit(solution)/shard_map/ppermute | solution.py:247
  37.5 9.0 %collective-permute-start.2 = (f32[136,1024]{1,0:T(8,128)S(1)}, f32[136,1024]{1,0:T(8,128)S(1)}, u32[]{:S(2)}, u32[]{:S(2)}) collective-permute-start(f32[136,1024]{1,0:T(8,128)S(1)} %collective-permute-done.refs_1_), channel_id=1, source_target_pairs={{0,28},{2,34},{4,0},{6,38},{8,4},{10,42},{12,8},{14,46},{16,12},{1... | collective-permute-start | bytes 1671176 | tf_op jit(solution)/shard_map/ppermute | solution.py:247
  46.5 4.0 %collective-permute-start.9 = (f32[136,1024]{1,0:T(8,128)S(1)}, f32[136,1024]{1,0:T(8,128)S(1)}, u32[]{:S(2)}, u32[]{:S(2)}) collective-permute-start(f32[136,1024]{1,0:T(8,128)S(1)} %collective-permute-done.2.refs_1_), channel_id=1, source_target_pairs={{0,2},{2,0},{4,6},{6,4},{8,10},{10,8},{12,14},{14,12},{16,18},{18,... | collective-permute-start | bytes 1671176 | tf_op jit(solution)/shard_map/ppermute | solution.py:247
  47.6 3.0 %collective-permute-start.8 = (f32[136,1024]{1,0:T(8,128)S(1)}, f32[136,1024]{1,0:T(8,128)S(1)}, u32[]{:S(2)}, u32[]{:S(2)}) collective-permute-start(f32[136,1024]{1,0:T(8,128)S(1)} %collective-permute-done.7.refs_0_), channel_id=1, source_target_pairs={{0,2},{2,0},{4,6},{6,4},{8,10},{10,8},{12,14},{14,12},{16,18},{18,... | collective-permute-start | bytes 1671176 | tf_op jit(solution)/shard_map/ppermute | solution.py:247
  47.6 10.2 %collective-permute-start.11 = (f32[136,1024]{1,0:T(8,128)S(1)}, f32[136,1024]{1,0:T(8,128)S(1)}, u32[]{:S(2)}, u32[]{:S(2)}) collective-permute-start(f32[136,1024]{1,0:T(8,128)S(1)} %collective-permute-done.7.refs_0_), channel_id=1, source_target_pairs={{0,4},{2,66},{4,8},{6,70},{8,12},{10,74},{12,16},{14,78},{16,20},{... | collective-permute-start | bytes 1671176 | tf_op jit(solution)/shard_map/ppermute | solution.py:247
  48.9 8.8 %collective-permute-start.6 = (f32[136,1024]{1,0:T(8,128)S(1)}, f32[136,1024]{1,0:T(8,128)S(1)}, u32[]{:S(2)}, u32[]{:S(2)}) collective-permute-start(f32[136,1024]{1,0:T(8,128)S(1)} %collective-permute-done.2.refs_1_), channel_id=1, source_target_pairs={{0,28},{2,34},{4,0},{6,38},{8,4},{10,42},{12,8},{14,46},{16,12},{1... | collective-permute-start | bytes 1671176 | tf_op jit(solution)/shard_map/ppermute | solution.py:247
  57.8 7.6 %collective-permute-start.13 = (f32[136,1024]{1,0:T(8,128)S(1)}, f32[136,1024]{1,0:T(8,128)S(1)}, u32[]{:S(2)}, u32[]{:S(2)}) collective-permute-start(f32[136,1024]{1,0:T(8,128)S(1)} %collective-permute-done.6.refs_1_), channel_id=1, source_target_pairs={{0,2},{2,0},{4,6},{6,4},{8,10},{10,8},{12,14},{14,12},{16,18},{18,... | collective-permute-start | bytes 1671176 | tf_op jit(solution)/shard_map/ppermute | solution.py:247
  59.5 5.8 %collective-permute-start.12 = (f32[136,1024]{1,0:T(8,128)S(1)}, f32[136,1024]{1,0:T(8,128)S(1)}, u32[]{:S(2)}, u32[]{:S(2)}) collective-permute-start(f32[136,1024]{1,0:T(8,128)S(1)} %collective-permute-done.11.refs_0_), channel_id=1, source_target_pairs={{0,2},{2,0},{4,6},{6,4},{8,10},{10,8},{12,14},{14,12},{16,18},{18,... | collective-permute-start | bytes 1671176 | tf_op jit(solution)/shard_map/ppermute | solution.py:247
  59.5 9.6 %collective-permute-start.10 = (f32[136,1024]{1,0:T(8,128)S(1)}, f32[136,1024]{1,0:T(8,128)S(1)}, u32[]{:S(2)}, u32[]{:S(2)}) collective-permute-start(f32[136,1024]{1,0:T(8,128)S(1)} %collective-permute-done.6.refs_1_), channel_id=1, source_target_pairs={{0,28},{2,34},{4,0},{6,38},{8,4},{10,42},{12,8},{14,46},{16,12},{1... | collective-permute-start | bytes 1671176 | tf_op jit(solution)/shard_map/ppermute | solution.py:247
  69.2 2.7 %collective-permute-start.14 = (f32[136,1024]{1,0:T(8,128)S(1)}, f32[136,1024]{1,0:T(8,128)S(1)}, u32[]{:S(2)}, u32[]{:S(2)}) collective-permute-start(f32[136,1024]{1,0:T(8,128)S(1)} %collective-permute-done.10.refs_0_), channel_id=1, source_target_pairs={{0,2},{2,0},{4,6},{6,4},{8,10},{10,8},{12,14},{14,12},{16,18},{18,... | collective-permute-start | bytes 1671176 | tf_op jit(solution)/shard_map/ppermute | solution.py:247

commit v4 on v3

--- a/solution.py
+++ b/solution.py
@@ -29,9 +29,9 @@
 LOOP = [(0, 0), (1, 0), (2, 0), (3, 0), (3, 1), (2, 1), (1, 1), (0, 1)]
 
 
-def ring(step):
+def ring(step, along_z=0):
     def target(x, y, z, c):
-        if c == 0:
+        if c == along_z:
             return x, y, z + step, c
         yh, yl = y // 2, y % 2
         nx, nh = LOOP[(LOOP.index(((x + 2 * yl) % 4, yh)) + step) % 8]
@@ -40,6 +40,7 @@
 
 
 FORWARD, BACKWARD = ring(1), ring(-1)
+OTHER_FORWARD = ring(1, along_z=1)
 SWAP = pairs(lambda x, y, z, c: (x, y, z, 1 - c))
 FIRST = [[flat(x, y, z, 0) for x in range(4) for y in range(4)] for z in range(8)] + [
     [flat(x, 2 * yh + yl, z, 1) for z in range(8) for yl in range(2)] for x in range(4) for yh in range(2)
@@ -112,10 +113,12 @@
 
 def join_kernel(parts, joined):
     count, n, width = parts.shape
-    rows, d = count * n, joined.shape[1]
-    joined[pl.ds(0, rows), :] = parts[:, :, :d].reshape(rows, d)
-    norms = jnp.transpose(parts[:, :, d:].reshape(rows, LANES))[:MARGIN, :]
-    joined[pl.ds(rows, MARGIN), :] = jnp.concatenate([norms, jnp.zeros((MARGIN, d - rows), f32)], axis=1)
+    rows = count * n
+    groups = width // LANES - 1
+    for i in range(groups):
+        joined[pl.ds(i * rows, rows), :] = parts[:, :, i * LANES : (i + 1) * LANES].reshape(rows, LANES)
+    norms = parts[:, :, groups * LANES :].reshape(rows, LANES)
+    joined[pl.ds(groups * rows, MARGIN), :] = jnp.transpose(norms)[:MARGIN, :]
 
 
 def join(parts):
@@ -124,7 +127,7 @@
         join_kernel,
         in_specs=[VMEM],
         out_specs=VMEM,
-        out_shape=pltpu.VMEM((count * n + MARGIN, width - LANES), f32),
+        out_shape=pltpu.VMEM((count * n * (width // LANES - 1) + MARGIN, LANES), f32),
         name="join",
     )(in_vmem(parts))
 
@@ -136,15 +139,12 @@
 def load_rows(blocks, row_high, row_low):
     norms = []
     for i, block in enumerate(blocks):
-        n = block.shape[0] - MARGIN
-        at = pl.ds(i * n, n)
-        row_high[at, :], row_low[at, :] = halves(block[:n, :])
-        norms.append(block[n : n + 1, :n])
+        size = block.shape[0] - MARGIN
+        rows = jnp.concatenate([block[j : j + LANES, :] for j in range(0, size, LANES)], axis=1)
+        at = pl.ds(i * LANES, LANES)
+        row_high[at, :], row_low[at, :] = halves(rows)
+        norms.append(block[size : size + 1, :])
     return jnp.concatenate(norms, axis=1)
-
-
-def rows_in(blocks):
-    return sum(b.shape[0] - MARGIN for b in blocks)
 
 
 def respond(high, low, penalty, norms, row_high, row_low, resp_high, resp_low, at):
@@ -184,7 +184,7 @@
 
 def chunk(blocks, high, low, penalty, sums):
     k, d = high.shape
-    count, rows = len(blocks), rows_in(blocks)
+    count, rows = len(blocks), LANES * len(blocks)
     args = [*blocks, high, low, penalty, *sums]
     return pl.pallas_call(
         functools.partial(chunk_kernel, count, not sums, 512),
@@ -223,7 +223,7 @@
 def last(blocks, high, low, penalty, sums):
     k, d = high.shape
     step, out_step = 512, 128
-    count, rows = len(blocks), rows_in(blocks)
+    count, rows = len(blocks), LANES * len(blocks)
     args = [*blocks, high, low, penalty, *sums]
     numerator, weights = pl.pallas_call(
         functools.partial(last_kernel, count, step, out_step),
@@ -253,17 +253,17 @@
     sums = chunk([own, send(own, SWAP)], *prepared, ())
     for _ in range(2):
         up, down, sums = after(up, sums), after(down, sums), after(sums, (up, down))
-        blocks = [after(up, down), after(down, up)]
+        blocks = [up, down]
         up, down = send(up, FORWARD), send(down, BACKWARD)
         sums = chunk(blocks + [send(b, SWAP) for b in blocks], *prepared, sums)
     up, down, sums = after(up, sums), after(down, sums), after(sums, (up, down))
     far = send(down, BACKWARD)
-    up, down = after(up, down), after(down, up)
     swapped = [send(up, SWAP), send(down, SWAP)]
-    sums = chunk([up, down], *prepared, sums)
-    sums = chunk(swapped, *prepared, sums)
-    far, sums = after(far, sums), after(sums, far)
-    return last([far, send(far, SWAP)], *prepared, sums)
+    other_far = send(swapped[0], OTHER_FORWARD)
+    sums = chunk([up, swapped[0]], *prepared, sums)
+    sums = chunk([down, swapped[1]], *prepared, sums)
+    far, other_far, sums = lax.optimization_barrier((far, other_far, sums))
+    return last([far, other_far], *prepared, sums)
 
 
 def solution(mesh):

time: 77.8 us -> 76.2 us (0.979)
  starting transfers between devices: 16.3 us -> 15 us
    ppermute x15, starting transfers between devices: 16.3 us -> 15 us  [send(): return lax.ppermute(v, AXES, how)]
  transfers between devices with their start and end apart: 15 -> 15, of which waited for: 2 -> 2; matrix products, arithmetic and copies ran while one was open for 0% -> 0% of each run, Pallas kernels for 36% -> 37%
where the time goes in v4:
time: 76.2 us; the launch traced here: 76 us
  Pallas kernels  33.9 us (44%)
  blocking collectives  23.4 us (31%)
  starting transfers between devices  15 us (20%)
  waiting for transfers between devices  2.03 us (3%)
  between operations  0.92 us (1%)
    pallas_call x5, Pallas kernels, chunk(): pl.pallas_call(functools.partial(chunk_kernel, count, not sums, 512), in_...  25.6 us
    all_to_all x1, blocking collectives, body(): lax.all_to_all(pack(rows, lognorm, 16), AXES, 0, 0, axis_index_groups=FIR...  23.4 us
    ppermute x15, starting transfers between devices, send(): return lax.ppermute(v, AXES, how)  15 us
    pallas_call x1, Pallas kernels, last(): pl.pallas_call(functools.partial(last_kernel, count, step, out_step), in_...  5.03 us
    pallas_call x1, Pallas kernels, prepare(): pl.pallas_call(functools.partial(prepare_kernel, parts), in_specs=[pl.Blo...  2.31 us
    ppermute x15, waiting for transfers between devices, send(): return lax.ppermute(v, AXES, how)  2.03 us
  transfers between devices with their start and end apart: 15, of which 2 were waited for; matrix products, arithmetic and copies ran while one was open for 0% of the time, Pallas kernels for 37%

profile of v4, /device:TPU:1, one launch (start us, length us, event | category | flops | bytes accessed | tf_op | source)
XLA Modules:
  0.0 76.0 jit_solution(9667002578302533380)
XLA Ops:
  0.6 0.8 %pack.1 = f32[16,8,1152]{2,1,0:T(8,128)S(1)} custom-call(f32[8,1024]{1,0:T(8,128)} %rows.1, f32[1,8]{1,0:T(1,128)} %bitcast.4), custom_call_target="tpu_custom_call" | custom-call | tf_op jit(solution)/shard_map/pack/pallas_call | solution.py:102
  1.5 23.4 %all_to_all.5.parts = f32[16,8,1152]{2,1,0:T(8,128)S(1)} all-to-all(f32[16,8,1152]{2,1,0:T(8,128)S(1)} %pack.1), channel_id=1, replica_groups={{0,1,32,33,64,65,96,97,128,129,160,161,192,193,224,225},{4,5,36,37,68,6..., dimensions={0} | all-to-all | bytes 1179648 | tf_op jit(solution)/shard_map/all_to_all | solution.py:249
  24.9 0.1 join.1.refs_0_
  25.1 1.3 %collective-permute-start.3 = (f32[1032,128]{1,0:T(8,128)S(1)}, f32[1032,128]{1,0:T(8,128)S(1)}, u32[]{:S(2)}, u32[]{:S(2)}) collective-permute-start(f32[1032,128]{1,0:T(8,128)S(1)} %join.1.refs_0_), channel_id=1, source_target_pairs={{0,4},{2,66},{4,8},{6,70},{8,12},{10,74},{12,16},{14,78},{16,20},{... | collective-permute-start | bytes 1585160 | tf_op jit(solution)/shard_map/ppermute | solution.py:247
  26.3 1.8 %collective-permute-start = (f32[1032,128]{1,0:T(8,128)S(1)}, f32[1032,128]{1,0:T(8,128)S(1)}, u32[]{:S(2)}, u32[]{:S(2)}) collective-permute-start(f32[1032,128]{1,0:T(8,128)S(1)} %join.1.refs_0_), channel_id=1, source_target_pairs={{0,28},{2,34},{4,0},{6,38},{8,4},{10,42},{12,8},{14,46},{16,12},{1... | collective-permute-start | bytes 1585160 | tf_op jit(solution)/shard_map/ppermute | solution.py:247
  28.1 0.7 copy-done
  28.8 2.3 %prepare.1 = (bf16[1024,1024]{1,0:T(8,128)(2,1)S(1)}, bf16[1024,1024]{1,0:T(8,128)(2,1)S(1)}, f32[1024,128]{1,0:T(8,128)S(1)}) custom-call(f32[1024,1024]{1,0:T(8,128)} %shard.1, s32[8,128]{1,0:T(8,128)S(1)} %bitcast.3), custom_call_target="tpu_custom_call" | custom-call | flops 4194304 | bytes 8388608 | tf_op jit(solution)/shard_map/prepare/pallas_call | solution.py:80
  31.1 3.5 %chunk.5 = (f32[1024,1024]{1,0:T(8,128)S(1)}, f32[1024,128]{1,0:T(8,128)S(1)}) custom-call(f32[1032,128]{1,0:T(8,128)S(1)} %join.1.refs_0_, f32[1032,128]{1,0:T(8,128)S(1)} %collective-permute-done.1.refs_1_, bf16[1024,1024]{1,0:T(8,128)(2,1)S(1)} %get-tuple-element.33.refs_2_.refs_4_, bf16[1024,1024]{1,0:T(8,128)(2,1)S(1)} %get-tuple-element.34.refs_3_.refs_5_, ...), custom_call_target="tpu_custom_call" | custom-call | flops 3221225472 | bytes 1048576 | tf_op jit(solution)/shard_map/chunk/pallas_call | solution.py:189
  34.7 1.3 %collective-permute-start.4 = (f32[1032,128]{1,0:T(8,128)S(1)}, f32[1032,128]{1,0:T(8,128)S(1)}, u32[]{:S(2)}, u32[]{:S(2)}) collective-permute-start(f32[1032,128]{1,0:T(8,128)S(1)} %collective-permute-done.3.refs_0_), channel_id=1, source_target_pairs={{0,2},{2,0},{4,6},{6,4},{8,10},{10,8},{12,14},{14,12},{16,18},{18,... | collective-permute-start | bytes 1585160 | tf_op jit(solution)/shard_map/ppermute | solution.py:247
  36.0 1.2 %collective-permute-start.7 = (f32[1032,128]{1,0:T(8,128)S(1)}, f32[1032,128]{1,0:T(8,128)S(1)}, u32[]{:S(2)}, u32[]{:S(2)}) collective-permute-start(f32[1032,128]{1,0:T(8,128)S(1)} %collective-permute-done.3.refs_0_), channel_id=1, source_target_pairs={{0,4},{2,66},{4,8},{6,70},{8,12},{10,74},{12,16},{14,78},{16,20},{... | collective-permute-start | bytes 1585160 | tf_op jit(solution)/shard_map/ppermute | solution.py:247
  37.2 1.8 %collective-permute-start.2 = (f32[1032,128]{1,0:T(8,128)S(1)}, f32[1032,128]{1,0:T(8,128)S(1)}, u32[]{:S(2)}, u32[]{:S(2)}) collective-permute-start(f32[1032,128]{1,0:T(8,128)S(1)} %collective-permute-done.refs_1_), channel_id=1, source_target_pairs={{0,28},{2,34},{4,0},{6,38},{8,4},{10,42},{12,8},{14,46},{16,12},{1... | collective-permute-start | bytes 1585160 | tf_op jit(solution)/shard_map/ppermute | solution.py:247
  39.0 7.2 %chunk.6 = (f32[1024,1024]{1,0:T(8,128)S(1)}, f32[1024,128]{1,0:T(8,128)S(1)}) custom-call(f32[1032,128]{1,0:T(8,128)S(1)} %collective-permute-done.3.refs_0_, f32[1032,128]{1,0:T(8,128)S(1)} %collective-permute-done.refs_1_, f32[1032,128]{1,0:T(8,128)S(1)} %collective-permute-done.4.refs_2_, ...), custom_call_target="tpu_custom_call", output_to_operand_aliasing={{0}: (7, {}), {1}: (8, {})} | custom-call | flops 6442450944 | bytes 2097152 | tf_op jit(solution)/shard_map/chunk/pallas_call | solution.py:189
  46.2 0.9 %collective-permute-start.8 = (f32[1032,128]{1,0:T(8,128)S(1)}, f32[1032,128]{1,0:T(8,128)S(1)}, u32[]{:S(2)}, u32[]{:S(2)}) collective-permute-start(f32[1032,128]{1,0:T(8,128)S(1)} %collective-permute-done.7.refs_0_), channel_id=1, source_target_pairs={{0,2},{2,0},{4,6},{6,4},{8,10},{10,8},{12,14},{14,12},{16,18},{18,... | collective-permute-start | bytes 1585160 | tf_op jit(solution)/shard_map/ppermute | solution.py:247
  47.1 0.1 collective-permute-start.9
  47.2 1.2 %collective-permute-start.11 = (f32[1032,128]{1,0:T(8,128)S(1)}, f32[1032,128]{1,0:T(8,128)S(1)}, u32[]{:S(2)}, u32[]{:S(2)}) collective-permute-start(f32[1032,128]{1,0:T(8,128)S(1)} %collective-permute-done.7.refs_0_), channel_id=1, source_target_pairs={{0,4},{2,66},{4,8},{6,70},{8,12},{10,74},{12,16},{14,78},{16,20},{... | collective-permute-start | bytes 1585160 | tf_op jit(solution)/shard_map/ppermute | solution.py:247
  48.4 1.8 %collective-permute-start.6 = (f32[1032,128]{1,0:T(8,128)S(1)}, f32[1032,128]{1,0:T(8,128)S(1)}, u32[]{:S(2)}, u32[]{:S(2)}) collective-permute-start(f32[1032,128]{1,0:T(8,128)S(1)} %collective-permute-done.2.refs_1_), channel_id=1, source_target_pairs={{0,28},{2,34},{4,0},{6,38},{8,4},{10,42},{12,8},{14,46},{16,12},{1... | collective-permute-start | bytes 1585160 | tf_op jit(solution)/shard_map/ppermute | solution.py:247
  50.2 7.2 %chunk.7 = (f32[1024,1024]{1,0:T(8,128)S(1)}, f32[1024,128]{1,0:T(8,128)S(1)}) custom-call(f32[1032,128]{1,0:T(8,128)S(1)} %collective-permute-done.7.refs_0_, f32[1032,128]{1,0:T(8,128)S(1)} %collective-permute-done.2.refs_1_, f32[1032,128]{1,0:T(8,128)S(1)} %collective-permute-done.8.refs_2_, ...), custom_call_target="tpu_custom_call", output_to_operand_aliasing={{0}: (7, {}), {1}: (8, {})} | custom-call | flops 6442450944 | bytes 2097152 | tf_op jit(solution)/shard_map/chunk/pallas_call | solution.py:189
  57.4 1.0 %collective-permute-start.12 = (f32[1032,128]{1,0:T(8,128)S(1)}, f32[1032,128]{1,0:T(8,128)S(1)}, u32[]{:S(2)}, u32[]{:S(2)}) collective-permute-start(f32[1032,128]{1,0:T(8,128)S(1)} %collective-permute-done.11.refs_0_), channel_id=1, source_target_pairs={{0,2},{2,0},{4,6},{6,4},{8,10},{10,8},{12,14},{14,12},{16,18},{18,... | collective-permute-start | bytes 1585160 | tf_op jit(solution)/shard_map/ppermute | solution.py:247
  58.4 0.1 collective-permute-start.14
  58.5 2.6 %collective-permute-start.10 = (f32[1032,128]{1,0:T(8,128)S(1)}, f32[1032,128]{1,0:T(8,128)S(1)}, u32[]{:S(2)}, u32[]{:S(2)}) collective-permute-start(f32[1032,128]{1,0:T(8,128)S(1)} %collective-permute-done.6.refs_0_), channel_id=1, source_target_pairs={{0,28},{2,34},{4,0},{6,38},{8,4},{10,42},{12,8},{14,46},{16,12},{1... | collective-permute-start | bytes 1585160 | tf_op jit(solution)/shard_map/ppermute | solution.py:247
  61.2 3.8 %chunk.8 = (f32[1024,1024]{1,0:T(8,128)S(1)}, f32[1024,128]{1,0:T(8,128)S(1)}) custom-call(f32[1032,128]{1,0:T(8,128)S(1)} %collective-permute-done.11.refs_0_, f32[1032,128]{1,0:T(8,128)S(1)} %collective-permute-done.12.refs_1_, bf16[1024,1024]{1,0:T(8,128)(2,1)S(1)} %get-tuple-element.33.refs_2_.refs_4_, ...), custom_call_target="tpu_custom_call", output_to_operand_aliasing={{0}: (5, {}), {1}: (6, {})} | custom-call | flops 3221225472 | bytes 1048576 | tf_op jit(solution)/shard_map/chunk/pallas_call | solution.py:189
  65.0 3.8 %chunk.9 = (f32[1024,1024]{1,0:T(8,128)S(1)}, f32[1024,128]{1,0:T(8,128)S(1)}) custom-call(f32[1032,128]{1,0:T(8,128)S(1)} %collective-permute-done.6.refs_0_, f32[1032,128]{1,0:T(8,128)S(1)} %collective-permute-done.14.refs_1_, bf16[1024,1024]{1,0:T(8,128)(2,1)S(1)} %get-tuple-element.33.refs_2_.refs_4_, ...), custom_call_target="tpu_custom_call", output_to_operand_aliasing={{0}: (5, {}), {1}: (6, {})} | custom-call | flops 3221225472 | bytes 1048576 | tf_op jit(solution)/shard_map/chunk/pallas_call | solution.py:189
  68.8 1.9 %collective-permute-done.13.refs_1_ = f32[1032,128]{1,0:T(8,128)S(1)} collective-permute-done((f32[1032,128]{1,0:T(8,128)S(1)}, f32[1032,128]{1,0:T(8,128)S(1)}, u32[]{:S(2)}, u32[]{:S(2)}) %collective-permute-start.13) | collective-permute-done | bytes 528416 | tf_op jit(solution)/shard_map/ppermute | solution.py:247
  70.7 5.0 %last.1 = (f32[1024,1024]{1,0:T(8,128)}, f32[8,128]{1,0:T(8,128)}) custom-call(f32[1032,128]{1,0:T(8,128)S(1)} %collective-permute-done.10.refs_0_, f32[1032,128]{1,0:T(8,128)S(1)} %collective-permute-done.13.refs_1_, bf16[1024,1024]{1,0:T(8,128)(2,1)S(1)} %get-tuple-element.33.refs_2_.refs_4_, bf16[1024,1024]{1,0:T(8,128)(2,1)S(1)} %get-tuple-element.34.refs_3_.refs_5_, ...), custom_call_target="tpu_custom_call" | custom-call | flops 3221225472 | bytes 1048576 | tf_op jit(solution)/shard_map/last/pallas_call | solution.py:228
  (18 shorter events, 0.2 us)
Async XLA Ops:
  25.0 6.1 %collective-permute-start.1 = (f32[1032,128]{1,0:T(8,128)S(1)}, f32[1032,128]{1,0:T(8,128)S(1)}, u32[]{:S(2)}, u32[]{:S(2)}) collective-permute-start(f32[1032,128]{1,0:T(8,128)S(1)} %join.1.refs_0_), channel_id=1, source_target_pairs={{0,2},{2,0},{4,6},{6,4},{8,10},{10,8},{12,14},{14,12},{16,18},{18,... | collective-permute-start | bytes 1585160 | tf_op jit(solution)/shard_map/ppermute | solution.py:247
  25.1 9.7 %collective-permute-start.3 = (f32[1032,128]{1,0:T(8,128)S(1)}, f32[1032,128]{1,0:T(8,128)S(1)}, u32[]{:S(2)}, u32[]{:S(2)}) collective-permute-start(f32[1032,128]{1,0:T(8,128)S(1)} %join.1.refs_0_), channel_id=1, source_target_pairs={{0,4},{2,66},{4,8},{6,70},{8,12},{10,74},{12,16},{14,78},{16,20},{... | collective-permute-start | bytes 1585160 | tf_op jit(solution)/shard_map/ppermute | solution.py:247
  26.3 9.6 %collective-permute-start = (f32[1032,128]{1,0:T(8,128)S(1)}, f32[1032,128]{1,0:T(8,128)S(1)}, u32[]{:S(2)}, u32[]{:S(2)}) collective-permute-start(f32[1032,128]{1,0:T(8,128)S(1)} %join.1.refs_0_), channel_id=1, source_target_pairs={{0,28},{2,34},{4,0},{6,38},{8,4},{10,42},{12,8},{14,46},{16,12},{1... | collective-permute-start | bytes 1585160 | tf_op jit(solution)/shard_map/ppermute | solution.py:247
  28.1 0.7 copy-start
  34.7 4.3 %collective-permute-start.4 = (f32[1032,128]{1,0:T(8,128)S(1)}, f32[1032,128]{1,0:T(8,128)S(1)}, u32[]{:S(2)}, u32[]{:S(2)}) collective-permute-start(f32[1032,128]{1,0:T(8,128)S(1)} %collective-permute-done.3.refs_0_), channel_id=1, source_target_pairs={{0,2},{2,0},{4,6},{6,4},{8,10},{10,8},{12,14},{14,12},{16,18},{18,... | collective-permute-start | bytes 1585160 | tf_op jit(solution)/shard_map/ppermute | solution.py:247
  36.0 3.0 %collective-permute-start.5 = (f32[1032,128]{1,0:T(8,128)S(1)}, f32[1032,128]{1,0:T(8,128)S(1)}, u32[]{:S(2)}, u32[]{:S(2)}) collective-permute-start(f32[1032,128]{1,0:T(8,128)S(1)} %collective-permute-done.refs_1_), channel_id=1, source_target_pairs={{0,2},{2,0},{4,6},{6,4},{8,10},{10,8},{12,14},{14,12},{16,18},{18,... | collective-permute-start | bytes 1585160 | tf_op jit(solution)/shard_map/ppermute | solution.py:247
  36.0 10.2 %collective-permute-start.7 = (f32[1032,128]{1,0:T(8,128)S(1)}, f32[1032,128]{1,0:T(8,128)S(1)}, u32[]{:S(2)}, u32[]{:S(2)}) collective-permute-start(f32[1032,128]{1,0:T(8,128)S(1)} %collective-permute-done.3.refs_0_), channel_id=1, source_target_pairs={{0,4},{2,66},{4,8},{6,70},{8,12},{10,74},{12,16},{14,78},{16,20},{... | collective-permute-start | bytes 1585160 | tf_op jit(solution)/shard_map/ppermute | solution.py:247
  37.2 9.9 %collective-permute-start.2 = (f32[1032,128]{1,0:T(8,128)S(1)}, f32[1032,128]{1,0:T(8,128)S(1)}, u32[]{:S(2)}, u32[]{:S(2)}) collective-permute-start(f32[1032,128]{1,0:T(8,128)S(1)} %collective-permute-done.refs_1_), channel_id=1, source_target_pairs={{0,28},{2,34},{4,0},{6,38},{8,4},{10,42},{12,8},{14,46},{16,12},{1... | collective-permute-start | bytes 1585160 | tf_op jit(solution)/shard_map/ppermute | solution.py:247
  46.2 3.9 %collective-permute-start.8 = (f32[1032,128]{1,0:T(8,128)S(1)}, f32[1032,128]{1,0:T(8,128)S(1)}, u32[]{:S(2)}, u32[]{:S(2)}) collective-permute-start(f32[1032,128]{1,0:T(8,128)S(1)} %collective-permute-done.7.refs_0_), channel_id=1, source_target_pairs={{0,2},{2,0},{4,6},{6,4},{8,10},{10,8},{12,14},{14,12},{16,18},{18,... | collective-permute-start | bytes 1585160 | tf_op jit(solution)/shard_map/ppermute | solution.py:247
  47.1 3.1 %collective-permute-start.9 = (f32[1032,128]{1,0:T(8,128)S(1)}, f32[1032,128]{1,0:T(8,128)S(1)}, u32[]{:S(2)}, u32[]{:S(2)}) collective-permute-start(f32[1032,128]{1,0:T(8,128)S(1)} %collective-permute-done.2.refs_1_), channel_id=1, source_target_pairs={{0,2},{2,0},{4,6},{6,4},{8,10},{10,8},{12,14},{14,12},{16,18},{18,... | collective-permute-start | bytes 1585160 | tf_op jit(solution)/shard_map/ppermute | solution.py:247
  47.2 10.2 %collective-permute-start.11 = (f32[1032,128]{1,0:T(8,128)S(1)}, f32[1032,128]{1,0:T(8,128)S(1)}, u32[]{:S(2)}, u32[]{:S(2)}) collective-permute-start(f32[1032,128]{1,0:T(8,128)S(1)} %collective-permute-done.7.refs_0_), channel_id=1, source_target_pairs={{0,4},{2,66},{4,8},{6,70},{8,12},{10,74},{12,16},{14,78},{16,20},{... | collective-permute-start | bytes 1585160 | tf_op jit(solution)/shard_map/ppermute | solution.py:247
  48.4 10.0 %collective-permute-start.6 = (f32[1032,128]{1,0:T(8,128)S(1)}, f32[1032,128]{1,0:T(8,128)S(1)}, u32[]{:S(2)}, u32[]{:S(2)}) collective-permute-start(f32[1032,128]{1,0:T(8,128)S(1)} %collective-permute-done.2.refs_1_), channel_id=1, source_target_pairs={{0,28},{2,34},{4,0},{6,38},{8,4},{10,42},{12,8},{14,46},{16,12},{1... | collective-permute-start | bytes 1585160 | tf_op jit(solution)/shard_map/ppermute | solution.py:247
  57.4 3.7 %collective-permute-start.12 = (f32[1032,128]{1,0:T(8,128)S(1)}, f32[1032,128]{1,0:T(8,128)S(1)}, u32[]{:S(2)}, u32[]{:S(2)}) collective-permute-start(f32[1032,128]{1,0:T(8,128)S(1)} %collective-permute-done.11.refs_0_), channel_id=1, source_target_pairs={{0,2},{2,0},{4,6},{6,4},{8,10},{10,8},{12,14},{14,12},{16,18},{18,... | collective-permute-start | bytes 1585160 | tf_op jit(solution)/shard_map/ppermute | solution.py:247
  58.4 6.6 %collective-permute-start.14 = (f32[1032,128]{1,0:T(8,128)S(1)}, f32[1032,128]{1,0:T(8,128)S(1)}, u32[]{:S(2)}, u32[]{:S(2)}) collective-permute-start(f32[1032,128]{1,0:T(8,128)S(1)} %collective-permute-done.6.refs_0_), channel_id=1, source_target_pairs={{0,2},{2,0},{4,6},{6,4},{8,10},{10,8},{12,14},{14,12},{16,18},{18,... | collective-permute-start | bytes 1585160 | tf_op jit(solution)/shard_map/ppermute | solution.py:247
  58.5 10.3 %collective-permute-start.10 = (f32[1032,128]{1,0:T(8,128)S(1)}, f32[1032,128]{1,0:T(8,128)S(1)}, u32[]{:S(2)}, u32[]{:S(2)}) collective-permute-start(f32[1032,128]{1,0:T(8,128)S(1)} %collective-permute-done.6.refs_0_), channel_id=1, source_target_pairs={{0,28},{2,34},{4,0},{6,38},{8,4},{10,42},{12,8},{14,46},{16,12},{1... | collective-permute-start | bytes 1585160 | tf_op jit(solution)/shard_map/ppermute | solution.py:247
  61.2 9.6 %collective-permute-start.13 = (f32[1032,128]{1,0:T(8,128)S(1)}, f32[1032,128]{1,0:T(8,128)S(1)}, u32[]{:S(2)}, u32[]{:S(2)}) collective-permute-start(f32[1032,128]{1,0:T(8,128)S(1)} %collective-permute-done.12.refs_1_), channel_id=1, source_target_pairs={{0,64},{2,6},{4,68},{6,10},{8,72},{10,14},{12,76},{14,18},{16,80},... | collective-permute-start | bytes 1585160 | tf_op jit(solution)/shard_map/ppermute | solution.py:247

commit v5 on v4

--- a/solution.py
+++ b/solution.py
@@ -60,13 +60,16 @@
     return dot(a_high, b_high, dims) + dot(a_low, b_high, dims) + dot(a_high, b_low, dims)
 
 
-def prepare_kernel(parts, shard, counts, high, low, penalty, landed, sems):
+def prepare_kernel(parts, shard, counts, high, low, penalty, landed, sizes, sems):
+    first = pltpu.make_async_copy(counts, sizes, sems.at[parts])
+    first.start()
     n = shard.shape[0] // parts
     places = [pl.ds(i * n, n) for i in range(parts)]
     copies = [pltpu.make_async_copy(shard.at[at, :], landed.at[at, :], sems.at[i]) for i, at in enumerate(places)]
     for copy in copies:
         copy.start()
-    pen = 0.5 * jnp.log(1.0 + counts[...].astype(f32))
+    first.wait()
+    pen = 0.5 * jnp.log(1.0 + sizes[...].astype(f32))
     for i in range(pen.shape[0]):
         penalty[pl.ds(i * LANES, LANES), :] = jnp.transpose(jnp.broadcast_to(pen[i : i + 1, :], (LANES, LANES)))
     for copy, at in zip(copies, places):
@@ -79,14 +82,22 @@
     parts = 8
     return pl.pallas_call(
         functools.partial(prepare_kernel, parts),
-        in_specs=[pl.BlockSpec(memory_space=pl.ANY), VMEM],
+        in_specs=[pl.BlockSpec(memory_space=pl.ANY)] * 2,
         out_specs=[VMEM] * 3,
         out_shape=[pltpu.VMEM((k, d), bf16), pltpu.VMEM((k, d), bf16), pltpu.VMEM((k, LANES), f32)],
-        scratch_shapes=[pltpu.VMEM((k, d), f32), pltpu.SemaphoreType.DMA((parts,))],
+        scratch_shapes=[
+            pltpu.VMEM((k, d), f32),
+            pltpu.VMEM((k // LANES, LANES), jnp.int32),
+            pltpu.SemaphoreType.DMA((parts + 1,)),
+        ],
         compiler_params=pltpu.CompilerParams(vmem_limit_bytes=8 * 2**20),
         cost_estimate=pl.CostEstimate(flops=4 * k * d, bytes_accessed=8 * k * d, transcendentals=0),
         name="prepare",
-    )(pltpu.with_memory_space_constraint(shard, pltpu.HBM), counts.reshape(k // LANES, LANES))
+    )(in_hbm(shard), in_hbm(counts.reshape(k // LANES, LANES)))
+
+
+def in_hbm(v):
+    return pltpu.with_memory_space_constraint(v, pltpu.HBM)
 
 
 def pack_kernel(rows, norms, packed):
@@ -187,7 +198,7 @@
     count, rows = len(blocks), LANES * len(blocks)
     args = [*blocks, high, low, penalty, *sums]
     return pl.pallas_call(
-        functools.partial(chunk_kernel, count, not sums, 512),
+        functools.partial(chunk_kernel, count, not sums, min(k, 256 * count)),
         in_specs=[VMEM] * len(args),
         out_specs=[VMEM] * 2,
         out_shape=[pltpu.VMEM((k, d), f32), pltpu.VMEM((k, LANES), f32)],

time: 76.2 us -> 76 us (level)
  no operation moved by 1% of the time
where the time goes in v5:
time: 76 us; the launch traced here: 75.6 us
  Pallas kernels  33.6 us (44%)
  blocking collectives  23.4 us (31%)
  starting transfers between devices  15.3 us (20%)
  waiting for transfers between devices  2.36 us (3%)
  between operations  0.94 us (1%)
    pallas_call x5, Pallas kernels, chunk(): pl.pallas_call(functools.partial(chunk_kernel, count, not sums, min(k, 25...  25.3 us
    all_to_all x1, blocking collectives, body(): lax.all_to_all(pack(rows, lognorm, 16), AXES, 0, 0, axis_index_groups=FIR...  23.4 us
    ppermute x15, starting transfers between devices, send(): return lax.ppermute(v, AXES, how)  15.3 us
    pallas_call x1, Pallas kernels, last(): pl.pallas_call(functools.partial(last_kernel, count, step, out_step), in_...  5.03 us
    ppermute x15, waiting for transfers between devices, send(): return lax.ppermute(v, AXES, how)  2.36 us
    pallas_call x1, Pallas kernels, prepare(): pl.pallas_call(functools.partial(prepare_kernel, parts), in_specs=[pl.Blo...  2.33 us
  transfers between devices with their start and end apart: 15, of which 2 were waited for; matrix products, arithmetic and copies ran while one was open for 0% of the time, Pallas kernels for 37%

profile of v5, /device:TPU:1, one launch (start us, length us, event | category | flops | bytes accessed | tf_op | source)
XLA Modules:
  0.0 75.6 jit_solution(7905881247448762902)
XLA Ops:
  0.6 0.8 %pack.1 = f32[16,8,1152]{2,1,0:T(8,128)S(1)} custom-call(f32[8,1024]{1,0:T(8,128)} %rows.1, f32[1,8]{1,0:T(1,128)} %bitcast.4), custom_call_target="tpu_custom_call" | custom-call | tf_op jit(solution)/shard_map/pack/pallas_call | solution.py:113
  1.5 23.4 %all_to_all.5.parts = f32[16,8,1152]{2,1,0:T(8,128)S(1)} all-to-all(f32[16,8,1152]{2,1,0:T(8,128)S(1)} %pack.1), channel_id=1, replica_groups={{0,1,32,33,64,65,96,97,128,129,160,161,192,193,224,225},{4,5,36,37,68,6..., dimensions={0} | all-to-all | bytes 1179648 | tf_op jit(solution)/shard_map/all_to_all | solution.py:260
  25.1 1.3 %collective-permute-start.3 = (f32[1032,128]{1,0:T(8,128)S(1)}, f32[1032,128]{1,0:T(8,128)S(1)}, u32[]{:S(2)}, u32[]{:S(2)}) collective-permute-start(f32[1032,128]{1,0:T(8,128)S(1)} %join.1.refs_0_), channel_id=1, source_target_pairs={{0,4},{2,66},{4,8},{6,70},{8,12},{10,74},{12,16},{14,78},{16,20},{... | collective-permute-start | bytes 1585160 | tf_op jit(solution)/shard_map/ppermute | solution.py:258
  26.3 1.8 %collective-permute-start = (f32[1032,128]{1,0:T(8,128)S(1)}, f32[1032,128]{1,0:T(8,128)S(1)}, u32[]{:S(2)}, u32[]{:S(2)}) collective-permute-start(f32[1032,128]{1,0:T(8,128)S(1)} %join.1.refs_0_), channel_id=1, source_target_pairs={{0,28},{2,34},{4,0},{6,38},{8,4},{10,42},{12,8},{14,46},{16,12},{1... | collective-permute-start | bytes 1585160 | tf_op jit(solution)/shard_map/ppermute | solution.py:258
  28.1 2.3 %prepare.1 = (bf16[1024,1024]{1,0:T(8,128)(2,1)S(1)}, bf16[1024,1024]{1,0:T(8,128)(2,1)S(1)}, f32[1024,128]{1,0:T(8,128)S(1)}) custom-call(f32[1024,1024]{1,0:T(8,128)} %shard.1, s32[8,128]{1,0:T(8,128)} %bitcast.3), custom_call_target="tpu_custom_call" | custom-call | flops 4194304 | bytes 8388608 | tf_op jit(solution)/shard_map/prepare/pallas_call | solution.py:83
  30.4 3.5 %chunk.5 = (f32[1024,1024]{1,0:T(8,128)S(1)}, f32[1024,128]{1,0:T(8,128)S(1)}) custom-call(f32[1032,128]{1,0:T(8,128)S(1)} %join.1.refs_0_, f32[1032,128]{1,0:T(8,128)S(1)} %collective-permute-done.1.refs_1_, bf16[1024,1024]{1,0:T(8,128)(2,1)S(1)} %get-tuple-element.33.refs_2_.refs_4_, bf16[1024,1024]{1,0:T(8,128)(2,1)S(1)} %get-tuple-element.34.refs_3_.refs_5_, ...), custom_call_target="tpu_custom_call" | custom-call | flops 3221225472 | bytes 1048576 | tf_op jit(solution)/shard_map/chunk/pallas_call | solution.py:200
  34.0 0.7 collective-permute-done.3.refs_0_
  34.7 1.3 %collective-permute-start.4 = (f32[1032,128]{1,0:T(8,128)S(1)}, f32[1032,128]{1,0:T(8,128)S(1)}, u32[]{:S(2)}, u32[]{:S(2)}) collective-permute-start(f32[1032,128]{1,0:T(8,128)S(1)} %collective-permute-done.3.refs_0_), channel_id=1, source_target_pairs={{0,2},{2,0},{4,6},{6,4},{8,10},{10,8},{12,14},{14,12},{16,18},{18,... | collective-permute-start | bytes 1585160 | tf_op jit(solution)/shard_map/ppermute | solution.py:258
  36.0 1.2 %collective-permute-start.7 = (f32[1032,128]{1,0:T(8,128)S(1)}, f32[1032,128]{1,0:T(8,128)S(1)}, u32[]{:S(2)}, u32[]{:S(2)}) collective-permute-start(f32[1032,128]{1,0:T(8,128)S(1)} %collective-permute-done.3.refs_0_), channel_id=1, source_target_pairs={{0,4},{2,66},{4,8},{6,70},{8,12},{10,74},{12,16},{14,78},{16,20},{... | collective-permute-start | bytes 1585160 | tf_op jit(solution)/shard_map/ppermute | solution.py:258
  37.2 1.8 %collective-permute-start.2 = (f32[1032,128]{1,0:T(8,128)S(1)}, f32[1032,128]{1,0:T(8,128)S(1)}, u32[]{:S(2)}, u32[]{:S(2)}) collective-permute-start(f32[1032,128]{1,0:T(8,128)S(1)} %collective-permute-done.refs_1_), channel_id=1, source_target_pairs={{0,28},{2,34},{4,0},{6,38},{8,4},{10,42},{12,8},{14,46},{16,12},{1... | collective-permute-start | bytes 1585160 | tf_op jit(solution)/shard_map/ppermute | solution.py:258
  39.0 7.1 %chunk.6 = (f32[1024,1024]{1,0:T(8,128)S(1)}, f32[1024,128]{1,0:T(8,128)S(1)}) custom-call(f32[1032,128]{1,0:T(8,128)S(1)} %collective-permute-done.3.refs_0_, f32[1032,128]{1,0:T(8,128)S(1)} %collective-permute-done.refs_1_, f32[1032,128]{1,0:T(8,128)S(1)} %collective-permute-done.4.refs_2_, ...), custom_call_target="tpu_custom_call", output_to_operand_aliasing={{0}: (7, {}), {1}: (8, {})} | custom-call | flops 6442450944 | bytes 2097152 | tf_op jit(solution)/shard_map/chunk/pallas_call | solution.py:200
  46.1 0.9 %collective-permute-start.8 = (f32[1032,128]{1,0:T(8,128)S(1)}, f32[1032,128]{1,0:T(8,128)S(1)}, u32[]{:S(2)}, u32[]{:S(2)}) collective-permute-start(f32[1032,128]{1,0:T(8,128)S(1)} %collective-permute-done.7.refs_0_), channel_id=1, source_target_pairs={{0,2},{2,0},{4,6},{6,4},{8,10},{10,8},{12,14},{14,12},{16,18},{18,... | collective-permute-start | bytes 1585160 | tf_op jit(solution)/shard_map/ppermute | solution.py:258
  47.0 0.1 collective-permute-start.9
  47.1 1.2 %collective-permute-start.11 = (f32[1032,128]{1,0:T(8,128)S(1)}, f32[1032,128]{1,0:T(8,128)S(1)}, u32[]{:S(2)}, u32[]{:S(2)}) collective-permute-start(f32[1032,128]{1,0:T(8,128)S(1)} %collective-permute-done.7.refs_0_), channel_id=1, source_target_pairs={{0,4},{2,66},{4,8},{6,70},{8,12},{10,74},{12,16},{14,78},{16,20},{... | collective-permute-start | bytes 1585160 | tf_op jit(solution)/shard_map/ppermute | solution.py:258
  48.3 1.8 %collective-permute-start.6 = (f32[1032,128]{1,0:T(8,128)S(1)}, f32[1032,128]{1,0:T(8,128)S(1)}, u32[]{:S(2)}, u32[]{:S(2)}) collective-permute-start(f32[1032,128]{1,0:T(8,128)S(1)} %collective-permute-done.2.refs_1_), channel_id=1, source_target_pairs={{0,28},{2,34},{4,0},{6,38},{8,4},{10,42},{12,8},{14,46},{16,12},{1... | collective-permute-start | bytes 1585160 | tf_op jit(solution)/shard_map/ppermute | solution.py:258
  50.0 7.1 %chunk.7 = (f32[1024,1024]{1,0:T(8,128)S(1)}, f32[1024,128]{1,0:T(8,128)S(1)}) custom-call(f32[1032,128]{1,0:T(8,128)S(1)} %collective-permute-done.7.refs_0_, f32[1032,128]{1,0:T(8,128)S(1)} %collective-permute-done.2.refs_1_, f32[1032,128]{1,0:T(8,128)S(1)} %collective-permute-done.8.refs_2_, ...), custom_call_target="tpu_custom_call", output_to_operand_aliasing={{0}: (7, {}), {1}: (8, {})} | custom-call | flops 6442450944 | bytes 2097152 | tf_op jit(solution)/shard_map/chunk/pallas_call | solution.py:200
  57.2 0.8 %collective-permute-start.12 = (f32[1032,128]{1,0:T(8,128)S(1)}, f32[1032,128]{1,0:T(8,128)S(1)}, u32[]{:S(2)}, u32[]{:S(2)}) collective-permute-start(f32[1032,128]{1,0:T(8,128)S(1)} %collective-permute-done.11.refs_0_), channel_id=1, source_target_pairs={{0,2},{2,0},{4,6},{6,4},{8,10},{10,8},{12,14},{14,12},{16,18},{18,... | collective-permute-start | bytes 1585160 | tf_op jit(solution)/shard_map/ppermute | solution.py:258
  57.9 0.1 collective-permute-start.14
  58.0 2.6 %collective-permute-start.10 = (f32[1032,128]{1,0:T(8,128)S(1)}, f32[1032,128]{1,0:T(8,128)S(1)}, u32[]{:S(2)}, u32[]{:S(2)}) collective-permute-start(f32[1032,128]{1,0:T(8,128)S(1)} %collective-permute-done.6.refs_0_), channel_id=1, source_target_pairs={{0,28},{2,34},{4,0},{6,38},{8,4},{10,42},{12,8},{14,46},{16,12},{1... | collective-permute-start | bytes 1585160 | tf_op jit(solution)/shard_map/ppermute | solution.py:258
  60.7 0.5 collective-permute-start.13
  61.2 3.8 %chunk.8 = (f32[1024,1024]{1,0:T(8,128)S(1)}, f32[1024,128]{1,0:T(8,128)S(1)}) custom-call(f32[1032,128]{1,0:T(8,128)S(1)} %collective-permute-done.11.refs_0_, f32[1032,128]{1,0:T(8,128)S(1)} %collective-permute-done.12.refs_1_, bf16[1024,1024]{1,0:T(8,128)(2,1)S(1)} %get-tuple-element.33.refs_2_.refs_4_, ...), custom_call_target="tpu_custom_call", output_to_operand_aliasing={{0}: (5, {}), {1}: (6, {})} | custom-call | flops 3221225472 | bytes 1048576 | tf_op jit(solution)/shard_map/chunk/pallas_call | solution.py:200
  65.0 3.8 %chunk.9 = (f32[1024,1024]{1,0:T(8,128)S(1)}, f32[1024,128]{1,0:T(8,128)S(1)}) custom-call(f32[1032,128]{1,0:T(8,128)S(1)} %collective-permute-done.6.refs_0_, f32[1032,128]{1,0:T(8,128)S(1)} %collective-permute-done.14.refs_1_, bf16[1024,1024]{1,0:T(8,128)(2,1)S(1)} %get-tuple-element.33.refs_2_.refs_4_, ...), custom_call_target="tpu_custom_call", output_to_operand_aliasing={{0}: (5, {}), {1}: (6, {})} | custom-call | flops 3221225472 | bytes 1048576 | tf_op jit(solution)/shard_map/chunk/pallas_call | solution.py:200
  68.8 1.6 %collective-permute-done.13.refs_1_ = f32[1032,128]{1,0:T(8,128)S(1)} collective-permute-done((f32[1032,128]{1,0:T(8,128)S(1)}, f32[1032,128]{1,0:T(8,128)S(1)}, u32[]{:S(2)}, u32[]{:S(2)}) %collective-permute-start.13) | collective-permute-done | bytes 528416 | tf_op jit(solution)/shard_map/ppermute | solution.py:258
  70.4 5.0 %last.1 = (f32[1024,1024]{1,0:T(8,128)}, f32[8,128]{1,0:T(8,128)}) custom-call(f32[1032,128]{1,0:T(8,128)S(1)} %collective-permute-done.10.refs_0_, f32[1032,128]{1,0:T(8,128)S(1)} %collective-permute-done.13.refs_1_, bf16[1024,1024]{1,0:T(8,128)(2,1)S(1)} %get-tuple-element.33.refs_2_.refs_4_, bf16[1024,1024]{1,0:T(8,128)(2,1)S(1)} %get-tuple-element.34.refs_3_.refs_5_, ...), custom_call_target="tpu_custom_call" | custom-call | flops 3221225472 | bytes 1048576 | tf_op jit(solution)/shard_map/last/pallas_call | solution.py:239
  (16 shorter events, 0.2 us)
Async XLA Ops:
  25.0 5.5 %collective-permute-start.1 = (f32[1032,128]{1,0:T(8,128)S(1)}, f32[1032,128]{1,0:T(8,128)S(1)}, u32[]{:S(2)}, u32[]{:S(2)}) collective-permute-start(f32[1032,128]{1,0:T(8,128)S(1)} %join.1.refs_0_), channel_id=1, source_target_pairs={{0,2},{2,0},{4,6},{6,4},{8,10},{10,8},{12,14},{14,12},{16,18},{18,... | collective-permute-start | bytes 1585160 | tf_op jit(solution)/shard_map/ppermute | solution.py:258
  25.1 9.7 %collective-permute-start.3 = (f32[1032,128]{1,0:T(8,128)S(1)}, f32[1032,128]{1,0:T(8,128)S(1)}, u32[]{:S(2)}, u32[]{:S(2)}) collective-permute-start(f32[1032,128]{1,0:T(8,128)S(1)} %join.1.refs_0_), channel_id=1, source_target_pairs={{0,4},{2,66},{4,8},{6,70},{8,12},{10,74},{12,16},{14,78},{16,20},{... | collective-permute-start | bytes 1585160 | tf_op jit(solution)/shard_map/ppermute | solution.py:258
  26.3 9.6 %collective-permute-start = (f32[1032,128]{1,0:T(8,128)S(1)}, f32[1032,128]{1,0:T(8,128)S(1)}, u32[]{:S(2)}, u32[]{:S(2)}) collective-permute-start(f32[1032,128]{1,0:T(8,128)S(1)} %join.1.refs_0_), channel_id=1, source_target_pairs={{0,28},{2,34},{4,0},{6,38},{8,4},{10,42},{12,8},{14,46},{16,12},{1... | collective-permute-start | bytes 1585160 | tf_op jit(solution)/shard_map/ppermute | solution.py:258
  34.7 4.3 %collective-permute-start.4 = (f32[1032,128]{1,0:T(8,128)S(1)}, f32[1032,128]{1,0:T(8,128)S(1)}, u32[]{:S(2)}, u32[]{:S(2)}) collective-permute-start(f32[1032,128]{1,0:T(8,128)S(1)} %collective-permute-done.3.refs_0_), channel_id=1, source_target_pairs={{0,2},{2,0},{4,6},{6,4},{8,10},{10,8},{12,14},{14,12},{16,18},{18,... | collective-permute-start | bytes 1585160 | tf_op jit(solution)/shard_map/ppermute | solution.py:258
  36.0 3.0 %collective-permute-start.5 = (f32[1032,128]{1,0:T(8,128)S(1)}, f32[1032,128]{1,0:T(8,128)S(1)}, u32[]{:S(2)}, u32[]{:S(2)}) collective-permute-start(f32[1032,128]{1,0:T(8,128)S(1)} %collective-permute-done.refs_1_), channel_id=1, source_target_pairs={{0,2},{2,0},{4,6},{6,4},{8,10},{10,8},{12,14},{14,12},{16,18},{18,... | collective-permute-start | bytes 1585160 | tf_op jit(solution)/shard_map/ppermute | solution.py:258
  36.0 10.1 %collective-permute-start.7 = (f32[1032,128]{1,0:T(8,128)S(1)}, f32[1032,128]{1,0:T(8,128)S(1)}, u32[]{:S(2)}, u32[]{:S(2)}) collective-permute-start(f32[1032,128]{1,0:T(8,128)S(1)} %collective-permute-done.3.refs_0_), channel_id=1, source_target_pairs={{0,4},{2,66},{4,8},{6,70},{8,12},{10,74},{12,16},{14,78},{16,20},{... | collective-permute-start | bytes 1585160 | tf_op jit(solution)/shard_map/ppermute | solution.py:258
  37.2 9.7 %collective-permute-start.2 = (f32[1032,128]{1,0:T(8,128)S(1)}, f32[1032,128]{1,0:T(8,128)S(1)}, u32[]{:S(2)}, u32[]{:S(2)}) collective-permute-start(f32[1032,128]{1,0:T(8,128)S(1)} %collective-permute-done.refs_1_), channel_id=1, source_target_pairs={{0,28},{2,34},{4,0},{6,38},{8,4},{10,42},{12,8},{14,46},{16,12},{1... | collective-permute-start | bytes 1585160 | tf_op jit(solution)/shard_map/ppermute | solution.py:258
  46.1 4.0 %collective-permute-start.8 = (f32[1032,128]{1,0:T(8,128)S(1)}, f32[1032,128]{1,0:T(8,128)S(1)}, u32[]{:S(2)}, u32[]{:S(2)}) collective-permute-start(f32[1032,128]{1,0:T(8,128)S(1)} %collective-permute-done.7.refs_0_), channel_id=1, source_target_pairs={{0,2},{2,0},{4,6},{6,4},{8,10},{10,8},{12,14},{14,12},{16,18},{18,... | collective-permute-start | bytes 1585160 | tf_op jit(solution)/shard_map/ppermute | solution.py:258
  47.0 3.1 %collective-permute-start.9 = (f32[1032,128]{1,0:T(8,128)S(1)}, f32[1032,128]{1,0:T(8,128)S(1)}, u32[]{:S(2)}, u32[]{:S(2)}) collective-permute-start(f32[1032,128]{1,0:T(8,128)S(1)} %collective-permute-done.2.refs_1_), channel_id=1, source_target_pairs={{0,2},{2,0},{4,6},{6,4},{8,10},{10,8},{12,14},{14,12},{16,18},{18,... | collective-permute-start | bytes 1585160 | tf_op jit(solution)/shard_map/ppermute | solution.py:258
  47.1 10.1 %collective-permute-start.11 = (f32[1032,128]{1,0:T(8,128)S(1)}, f32[1032,128]{1,0:T(8,128)S(1)}, u32[]{:S(2)}, u32[]{:S(2)}) collective-permute-start(f32[1032,128]{1,0:T(8,128)S(1)} %collective-permute-done.7.refs_0_), channel_id=1, source_target_pairs={{0,4},{2,66},{4,8},{6,70},{8,12},{10,74},{12,16},{14,78},{16,20},{... | collective-permute-start | bytes 1585160 | tf_op jit(solution)/shard_map/ppermute | solution.py:258
  48.3 9.7 %collective-permute-start.6 = (f32[1032,128]{1,0:T(8,128)S(1)}, f32[1032,128]{1,0:T(8,128)S(1)}, u32[]{:S(2)}, u32[]{:S(2)}) collective-permute-start(f32[1032,128]{1,0:T(8,128)S(1)} %collective-permute-done.2.refs_1_), channel_id=1, source_target_pairs={{0,28},{2,34},{4,0},{6,38},{8,4},{10,42},{12,8},{14,46},{16,12},{1... | collective-permute-start | bytes 1585160 | tf_op jit(solution)/shard_map/ppermute | solution.py:258
  57.2 3.5 %collective-permute-start.12 = (f32[1032,128]{1,0:T(8,128)S(1)}, f32[1032,128]{1,0:T(8,128)S(1)}, u32[]{:S(2)}, u32[]{:S(2)}) collective-permute-start(f32[1032,128]{1,0:T(8,128)S(1)} %collective-permute-done.11.refs_0_), channel_id=1, source_target_pairs={{0,2},{2,0},{4,6},{6,4},{8,10},{10,8},{12,14},{14,12},{16,18},{18,... | collective-permute-start | bytes 1585160 | tf_op jit(solution)/shard_map/ppermute | solution.py:258
  57.9 7.0 %collective-permute-start.14 = (f32[1032,128]{1,0:T(8,128)S(1)}, f32[1032,128]{1,0:T(8,128)S(1)}, u32[]{:S(2)}, u32[]{:S(2)}) collective-permute-start(f32[1032,128]{1,0:T(8,128)S(1)} %collective-permute-done.6.refs_0_), channel_id=1, source_target_pairs={{0,2},{2,0},{4,6},{6,4},{8,10},{10,8},{12,14},{14,12},{16,18},{18,... | collective-permute-start | bytes 1585160 | tf_op jit(solution)/shard_map/ppermute | solution.py:258
  58.0 10.8 %collective-permute-start.10 = (f32[1032,128]{1,0:T(8,128)S(1)}, f32[1032,128]{1,0:T(8,128)S(1)}, u32[]{:S(2)}, u32[]{:S(2)}) collective-permute-start(f32[1032,128]{1,0:T(8,128)S(1)} %collective-permute-done.6.refs_0_), channel_id=1, source_target_pairs={{0,28},{2,34},{4,0},{6,38},{8,4},{10,42},{12,8},{14,46},{16,12},{1... | collective-permute-start | bytes 1585160 | tf_op jit(solution)/shard_map/ppermute | solution.py:258
  60.7 9.7 %collective-permute-start.13 = (f32[1032,128]{1,0:T(8,128)S(1)}, f32[1032,128]{1,0:T(8,128)S(1)}, u32[]{:S(2)}, u32[]{:S(2)}) collective-permute-start(f32[1032,128]{1,0:T(8,128)S(1)} %collective-permute-done.12.refs_1_), channel_id=1, source_target_pairs={{0,64},{2,6},{4,68},{6,10},{8,72},{10,14},{12,76},{14,18},{16,80},... | collective-permute-start | bytes 1585160 | tf_op jit(solution)/shard_map/ppermute | solution.py:258

commit v6 on v5

--- a/solution.py
+++ b/solution.py
@@ -190,7 +190,7 @@
 
 
 def cost(rows, k, d):
-    return pl.CostEstimate(flops=12 * rows * k * d, bytes_accessed=4 * rows * d, transcendentals=rows * k)
+    return pl.CostEstimate(flops=rows * k, bytes_accessed=rows, transcendentals=0)
 
 
 def chunk(blocks, high, low, penalty, sums):

time: 76 us -> 76 us (level)
  no operation moved by 1% of the time
where the time goes in v6:
time: 76 us; the launch traced here: 75.7 us
  Pallas kernels  33.7 us (44%)
  blocking collectives  23.4 us (31%)
  starting transfers between devices  15.3 us (20%)
  waiting for transfers between devices  2.34 us (3%)
  between operations  0.94 us (1%)
    pallas_call x5, Pallas kernels, chunk(): pl.pallas_call(functools.partial(chunk_kernel, count, not sums, min(k, 25...  25.4 us
    all_to_all x1, blocking collectives, body(): lax.all_to_all(pack(rows, lognorm, 16), AXES, 0, 0, axis_index_groups=FIR...  23.4 us
    ppermute x15, starting transfers between devices, send(): return lax.ppermute(v, AXES, how)  15.3 us
    pallas_call x1, Pallas kernels, last(): pl.pallas_call(functools.partial(last_kernel, count, step, out_step), in_...  5.04 us
    ppermute x15, waiting for transfers between devices, send(): return lax.ppermute(v, AXES, how)  2.34 us
    pallas_call x1, Pallas kernels, prepare(): pl.pallas_call(functools.partial(prepare_kernel, parts), in_specs=[pl.Blo...  2.33 us
  transfers between devices with their start and end apart: 15, of which 2 were waited for; matrix products, arithmetic and copies ran while one was open for 0% of the time, Pallas kernels for 37%

profile of v6, /device:TPU:1, one launch (start us, length us, event | category | flops | bytes accessed | tf_op | source)
XLA Modules:
  0.0 75.7 jit_solution(13363426066283651192)
XLA Ops:
  0.6 0.8 %pack.1 = f32[16,8,1152]{2,1,0:T(8,128)S(1)} custom-call(f32[8,1024]{1,0:T(8,128)} %rows.1, f32[1,8]{1,0:T(1,128)} %bitcast.4), custom_call_target="tpu_custom_call" | custom-call | tf_op jit(solution)/shard_map/pack/pallas_call | solution.py:113
  1.5 23.4 %all_to_all.5.parts = f32[16,8,1152]{2,1,0:T(8,128)S(1)} all-to-all(f32[16,8,1152]{2,1,0:T(8,128)S(1)} %pack.1), channel_id=1, replica_groups={{0,1,32,33,64,65,96,97,128,129,160,161,192,193,224,225},{4,5,36,37,68,6..., dimensions={0} | all-to-all | bytes 1179648 | tf_op jit(solution)/shard_map/all_to_all | solution.py:260
  25.1 1.3 %collective-permute-start.3 = (f32[1032,128]{1,0:T(8,128)S(1)}, f32[1032,128]{1,0:T(8,128)S(1)}, u32[]{:S(2)}, u32[]{:S(2)}) collective-permute-start(f32[1032,128]{1,0:T(8,128)S(1)} %join.1.refs_0_), channel_id=1, source_target_pairs={{0,4},{2,66},{4,8},{6,70},{8,12},{10,74},{12,16},{14,78},{16,20},{... | collective-permute-start | bytes 1585160 | tf_op jit(solution)/shard_map/ppermute | solution.py:258
  26.3 1.8 %collective-permute-start = (f32[1032,128]{1,0:T(8,128)S(1)}, f32[1032,128]{1,0:T(8,128)S(1)}, u32[]{:S(2)}, u32[]{:S(2)}) collective-permute-start(f32[1032,128]{1,0:T(8,128)S(1)} %join.1.refs_0_), channel_id=1, source_target_pairs={{0,28},{2,34},{4,0},{6,38},{8,4},{10,42},{12,8},{14,46},{16,12},{1... | collective-permute-start | bytes 1585160 | tf_op jit(solution)/shard_map/ppermute | solution.py:258
  28.1 2.3 %prepare.1 = (bf16[1024,1024]{1,0:T(8,128)(2,1)S(1)}, bf16[1024,1024]{1,0:T(8,128)(2,1)S(1)}, f32[1024,128]{1,0:T(8,128)S(1)}) custom-call(f32[1024,1024]{1,0:T(8,128)} %shard.1, s32[8,128]{1,0:T(8,128)} %bitcast.3), custom_call_target="tpu_custom_call" | custom-call | flops 4194304 | bytes 8388608 | tf_op jit(solution)/shard_map/prepare/pallas_call | solution.py:83
  30.4 3.6 %chunk.5 = (f32[1024,1024]{1,0:T(8,128)S(1)}, f32[1024,128]{1,0:T(8,128)S(1)}) custom-call(f32[1032,128]{1,0:T(8,128)S(1)} %join.1.refs_0_, f32[1032,128]{1,0:T(8,128)S(1)} %collective-permute-done.1.refs_1_, bf16[1024,1024]{1,0:T(8,128)(2,1)S(1)} %get-tuple-element.33.refs_2_.refs_4_, bf16[1024,1024]{1,0:T(8,128)(2,1)S(1)} %get-tuple-element.34.refs_3_.refs_5_, ...), custom_call_target="tpu_custom_call" | custom-call | flops 262144 | bytes 256 | tf_op jit(solution)/shard_map/chunk/pallas_call | solution.py:200
  34.0 0.7 collective-permute-done.3.refs_0_
  34.7 1.3 %collective-permute-start.4 = (f32[1032,128]{1,0:T(8,128)S(1)}, f32[1032,128]{1,0:T(8,128)S(1)}, u32[]{:S(2)}, u32[]{:S(2)}) collective-permute-start(f32[1032,128]{1,0:T(8,128)S(1)} %collective-permute-done.3.refs_0_), channel_id=1, source_target_pairs={{0,2},{2,0},{4,6},{6,4},{8,10},{10,8},{12,14},{14,12},{16,18},{18,... | collective-permute-start | bytes 1585160 | tf_op jit(solution)/shard_map/ppermute | solution.py:258
  36.0 1.2 %collective-permute-start.7 = (f32[1032,128]{1,0:T(8,128)S(1)}, f32[1032,128]{1,0:T(8,128)S(1)}, u32[]{:S(2)}, u32[]{:S(2)}) collective-permute-start(f32[1032,128]{1,0:T(8,128)S(1)} %collective-permute-done.3.refs_0_), channel_id=1, source_target_pairs={{0,4},{2,66},{4,8},{6,70},{8,12},{10,74},{12,16},{14,78},{16,20},{... | collective-permute-start | bytes 1585160 | tf_op jit(solution)/shard_map/ppermute | solution.py:258
  37.2 1.8 %collective-permute-start.2 = (f32[1032,128]{1,0:T(8,128)S(1)}, f32[1032,128]{1,0:T(8,128)S(1)}, u32[]{:S(2)}, u32[]{:S(2)}) collective-permute-start(f32[1032,128]{1,0:T(8,128)S(1)} %collective-permute-done.refs_1_), channel_id=1, source_target_pairs={{0,28},{2,34},{4,0},{6,38},{8,4},{10,42},{12,8},{14,46},{16,12},{1... | collective-permute-start | bytes 1585160 | tf_op jit(solution)/shard_map/ppermute | solution.py:258
  39.0 7.1 %chunk.6 = (f32[1024,1024]{1,0:T(8,128)S(1)}, f32[1024,128]{1,0:T(8,128)S(1)}) custom-call(f32[1032,128]{1,0:T(8,128)S(1)} %collective-permute-done.3.refs_0_, f32[1032,128]{1,0:T(8,128)S(1)} %collective-permute-done.refs_1_, f32[1032,128]{1,0:T(8,128)S(1)} %collective-permute-done.4.refs_2_, ...), custom_call_target="tpu_custom_call", output_to_operand_aliasing={{0}: (7, {}), {1}: (8, {})} | custom-call | flops 524288 | bytes 512 | tf_op jit(solution)/shard_map/chunk/pallas_call | solution.py:200
  46.1 0.9 %collective-permute-start.8 = (f32[1032,128]{1,0:T(8,128)S(1)}, f32[1032,128]{1,0:T(8,128)S(1)}, u32[]{:S(2)}, u32[]{:S(2)}) collective-permute-start(f32[1032,128]{1,0:T(8,128)S(1)} %collective-permute-done.7.refs_0_), channel_id=1, source_target_pairs={{0,2},{2,0},{4,6},{6,4},{8,10},{10,8},{12,14},{14,12},{16,18},{18,... | collective-permute-start | bytes 1585160 | tf_op jit(solution)/shard_map/ppermute | solution.py:258
  47.0 0.1 collective-permute-start.9
  47.1 1.2 %collective-permute-start.11 = (f32[1032,128]{1,0:T(8,128)S(1)}, f32[1032,128]{1,0:T(8,128)S(1)}, u32[]{:S(2)}, u32[]{:S(2)}) collective-permute-start(f32[1032,128]{1,0:T(8,128)S(1)} %collective-permute-done.7.refs_0_), channel_id=1, source_target_pairs={{0,4},{2,66},{4,8},{6,70},{8,12},{10,74},{12,16},{14,78},{16,20},{... | collective-permute-start | bytes 1585160 | tf_op jit(solution)/shard_map/ppermute | solution.py:258
  48.3 1.8 %collective-permute-start.6 = (f32[1032,128]{1,0:T(8,128)S(1)}, f32[1032,128]{1,0:T(8,128)S(1)}, u32[]{:S(2)}, u32[]{:S(2)}) collective-permute-start(f32[1032,128]{1,0:T(8,128)S(1)} %collective-permute-done.2.refs_1_), channel_id=1, source_target_pairs={{0,28},{2,34},{4,0},{6,38},{8,4},{10,42},{12,8},{14,46},{16,12},{1... | collective-permute-start | bytes 1585160 | tf_op jit(solution)/shard_map/ppermute | solution.py:258
  50.0 7.1 %chunk.7 = (f32[1024,1024]{1,0:T(8,128)S(1)}, f32[1024,128]{1,0:T(8,128)S(1)}) custom-call(f32[1032,128]{1,0:T(8,128)S(1)} %collective-permute-done.7.refs_0_, f32[1032,128]{1,0:T(8,128)S(1)} %collective-permute-done.2.refs_1_, f32[1032,128]{1,0:T(8,128)S(1)} %collective-permute-done.8.refs_2_, ...), custom_call_target="tpu_custom_call", output_to_operand_aliasing={{0}: (7, {}), {1}: (8, {})} | custom-call | flops 524288 | bytes 512 | tf_op jit(solution)/shard_map/chunk/pallas_call | solution.py:200
  57.2 0.8 %collective-permute-start.12 = (f32[1032,128]{1,0:T(8,128)S(1)}, f32[1032,128]{1,0:T(8,128)S(1)}, u32[]{:S(2)}, u32[]{:S(2)}) collective-permute-start(f32[1032,128]{1,0:T(8,128)S(1)} %collective-permute-done.11.refs_0_), channel_id=1, source_target_pairs={{0,2},{2,0},{4,6},{6,4},{8,10},{10,8},{12,14},{14,12},{16,18},{18,... | collective-permute-start | bytes 1585160 | tf_op jit(solution)/shard_map/ppermute | solution.py:258
  57.9 0.1 collective-permute-start.14
  58.1 2.6 %collective-permute-start.10 = (f32[1032,128]{1,0:T(8,128)S(1)}, f32[1032,128]{1,0:T(8,128)S(1)}, u32[]{:S(2)}, u32[]{:S(2)}) collective-permute-start(f32[1032,128]{1,0:T(8,128)S(1)} %collective-permute-done.6.refs_0_), channel_id=1, source_target_pairs={{0,28},{2,34},{4,0},{6,38},{8,4},{10,42},{12,8},{14,46},{16,12},{1... | collective-permute-start | bytes 1585160 | tf_op jit(solution)/shard_map/ppermute | solution.py:258
  60.7 0.5 collective-permute-start.13
  61.2 3.8 %chunk.8 = (f32[1024,1024]{1,0:T(8,128)S(1)}, f32[1024,128]{1,0:T(8,128)S(1)}) custom-call(f32[1032,128]{1,0:T(8,128)S(1)} %collective-permute-done.11.refs_0_, f32[1032,128]{1,0:T(8,128)S(1)} %collective-permute-done.12.refs_1_, bf16[1024,1024]{1,0:T(8,128)(2,1)S(1)} %get-tuple-element.33.refs_2_.refs_4_, ...), custom_call_target="tpu_custom_call", output_to_operand_aliasing={{0}: (5, {}), {1}: (6, {})} | custom-call | flops 262144 | bytes 256 | tf_op jit(solution)/shard_map/chunk/pallas_call | solution.py:200
  65.0 3.8 %chunk.9 = (f32[1024,1024]{1,0:T(8,128)S(1)}, f32[1024,128]{1,0:T(8,128)S(1)}) custom-call(f32[1032,128]{1,0:T(8,128)S(1)} %collective-permute-done.6.refs_0_, f32[1032,128]{1,0:T(8,128)S(1)} %collective-permute-done.14.refs_1_, bf16[1024,1024]{1,0:T(8,128)(2,1)S(1)} %get-tuple-element.33.refs_2_.refs_4_, ...), custom_call_target="tpu_custom_call", output_to_operand_aliasing={{0}: (5, {}), {1}: (6, {})} | custom-call | flops 262144 | bytes 256 | tf_op jit(solution)/shard_map/chunk/pallas_call | solution.py:200
  68.8 1.6 %collective-permute-done.13.refs_1_ = f32[1032,128]{1,0:T(8,128)S(1)} collective-permute-done((f32[1032,128]{1,0:T(8,128)S(1)}, f32[1032,128]{1,0:T(8,128)S(1)}, u32[]{:S(2)}, u32[]{:S(2)}) %collective-permute-start.13) | collective-permute-done | bytes 528416 | tf_op jit(solution)/shard_map/ppermute | solution.py:258
  70.4 5.0 %last.1 = (f32[1024,1024]{1,0:T(8,128)}, f32[8,128]{1,0:T(8,128)}) custom-call(f32[1032,128]{1,0:T(8,128)S(1)} %collective-permute-done.10.refs_0_, f32[1032,128]{1,0:T(8,128)S(1)} %collective-permute-done.13.refs_1_, bf16[1024,1024]{1,0:T(8,128)(2,1)S(1)} %get-tuple-element.33.refs_2_.refs_4_, bf16[1024,1024]{1,0:T(8,128)(2,1)S(1)} %get-tuple-element.34.refs_3_.refs_5_, ...), custom_call_target="tpu_custom_call" | custom-call | flops 262144 | bytes 256 | tf_op jit(solution)/shard_map/last/pallas_call | solution.py:239
  (16 shorter events, 0.2 us)
Async XLA Ops:
  25.0 5.5 %collective-permute-start.1 = (f32[1032,128]{1,0:T(8,128)S(1)}, f32[1032,128]{1,0:T(8,128)S(1)}, u32[]{:S(2)}, u32[]{:S(2)}) collective-permute-start(f32[1032,128]{1,0:T(8,128)S(1)} %join.1.refs_0_), channel_id=1, source_target_pairs={{0,2},{2,0},{4,6},{6,4},{8,10},{10,8},{12,14},{14,12},{16,18},{18,... | collective-permute-start | bytes 1585160 | tf_op jit(solution)/shard_map/ppermute | solution.py:258
  25.1 9.7 %collective-permute-start.3 = (f32[1032,128]{1,0:T(8,128)S(1)}, f32[1032,128]{1,0:T(8,128)S(1)}, u32[]{:S(2)}, u32[]{:S(2)}) collective-permute-start(f32[1032,128]{1,0:T(8,128)S(1)} %join.1.refs_0_), channel_id=1, source_target_pairs={{0,4},{2,66},{4,8},{6,70},{8,12},{10,74},{12,16},{14,78},{16,20},{... | collective-permute-start | bytes 1585160 | tf_op jit(solution)/shard_map/ppermute | solution.py:258
  26.3 9.6 %collective-permute-start = (f32[1032,128]{1,0:T(8,128)S(1)}, f32[1032,128]{1,0:T(8,128)S(1)}, u32[]{:S(2)}, u32[]{:S(2)}) collective-permute-start(f32[1032,128]{1,0:T(8,128)S(1)} %join.1.refs_0_), channel_id=1, source_target_pairs={{0,28},{2,34},{4,0},{6,38},{8,4},{10,42},{12,8},{14,46},{16,12},{1... | collective-permute-start | bytes 1585160 | tf_op jit(solution)/shard_map/ppermute | solution.py:258
  34.7 4.3 %collective-permute-start.4 = (f32[1032,128]{1,0:T(8,128)S(1)}, f32[1032,128]{1,0:T(8,128)S(1)}, u32[]{:S(2)}, u32[]{:S(2)}) collective-permute-start(f32[1032,128]{1,0:T(8,128)S(1)} %collective-permute-done.3.refs_0_), channel_id=1, source_target_pairs={{0,2},{2,0},{4,6},{6,4},{8,10},{10,8},{12,14},{14,12},{16,18},{18,... | collective-permute-start | bytes 1585160 | tf_op jit(solution)/shard_map/ppermute | solution.py:258
  36.0 3.0 %collective-permute-start.5 = (f32[1032,128]{1,0:T(8,128)S(1)}, f32[1032,128]{1,0:T(8,128)S(1)}, u32[]{:S(2)}, u32[]{:S(2)}) collective-permute-start(f32[1032,128]{1,0:T(8,128)S(1)} %collective-permute-done.refs_1_), channel_id=1, source_target_pairs={{0,2},{2,0},{4,6},{6,4},{8,10},{10,8},{12,14},{14,12},{16,18},{18,... | collective-permute-start | bytes 1585160 | tf_op jit(solution)/shard_map/ppermute | solution.py:258
  36.0 10.1 %collective-permute-start.7 = (f32[1032,128]{1,0:T(8,128)S(1)}, f32[1032,128]{1,0:T(8,128)S(1)}, u32[]{:S(2)}, u32[]{:S(2)}) collective-permute-start(f32[1032,128]{1,0:T(8,128)S(1)} %collective-permute-done.3.refs_0_), channel_id=1, source_target_pairs={{0,4},{2,66},{4,8},{6,70},{8,12},{10,74},{12,16},{14,78},{16,20},{... | collective-permute-start | bytes 1585160 | tf_op jit(solution)/shard_map/ppermute | solution.py:258
  37.2 9.8 %collective-permute-start.2 = (f32[1032,128]{1,0:T(8,128)S(1)}, f32[1032,128]{1,0:T(8,128)S(1)}, u32[]{:S(2)}, u32[]{:S(2)}) collective-permute-start(f32[1032,128]{1,0:T(8,128)S(1)} %collective-permute-done.refs_1_), channel_id=1, source_target_pairs={{0,28},{2,34},{4,0},{6,38},{8,4},{10,42},{12,8},{14,46},{16,12},{1... | collective-permute-start | bytes 1585160 | tf_op jit(solution)/shard_map/ppermute | solution.py:258
  46.1 3.9 %collective-permute-start.8 = (f32[1032,128]{1,0:T(8,128)S(1)}, f32[1032,128]{1,0:T(8,128)S(1)}, u32[]{:S(2)}, u32[]{:S(2)}) collective-permute-start(f32[1032,128]{1,0:T(8,128)S(1)} %collective-permute-done.7.refs_0_), channel_id=1, source_target_pairs={{0,2},{2,0},{4,6},{6,4},{8,10},{10,8},{12,14},{14,12},{16,18},{18,... | collective-permute-start | bytes 1585160 | tf_op jit(solution)/shard_map/ppermute | solution.py:258
  47.0 3.1 %collective-permute-start.9 = (f32[1032,128]{1,0:T(8,128)S(1)}, f32[1032,128]{1,0:T(8,128)S(1)}, u32[]{:S(2)}, u32[]{:S(2)}) collective-permute-start(f32[1032,128]{1,0:T(8,128)S(1)} %collective-permute-done.2.refs_1_), channel_id=1, source_target_pairs={{0,2},{2,0},{4,6},{6,4},{8,10},{10,8},{12,14},{14,12},{16,18},{18,... | collective-permute-start | bytes 1585160 | tf_op jit(solution)/shard_map/ppermute | solution.py:258
  47.1 10.1 %collective-permute-start.11 = (f32[1032,128]{1,0:T(8,128)S(1)}, f32[1032,128]{1,0:T(8,128)S(1)}, u32[]{:S(2)}, u32[]{:S(2)}) collective-permute-start(f32[1032,128]{1,0:T(8,128)S(1)} %collective-permute-done.7.refs_0_), channel_id=1, source_target_pairs={{0,4},{2,66},{4,8},{6,70},{8,12},{10,74},{12,16},{14,78},{16,20},{... | collective-permute-start | bytes 1585160 | tf_op jit(solution)/shard_map/ppermute | solution.py:258
  48.3 9.7 %collective-permute-start.6 = (f32[1032,128]{1,0:T(8,128)S(1)}, f32[1032,128]{1,0:T(8,128)S(1)}, u32[]{:S(2)}, u32[]{:S(2)}) collective-permute-start(f32[1032,128]{1,0:T(8,128)S(1)} %collective-permute-done.2.refs_1_), channel_id=1, source_target_pairs={{0,28},{2,34},{4,0},{6,38},{8,4},{10,42},{12,8},{14,46},{16,12},{1... | collective-permute-start | bytes 1585160 | tf_op jit(solution)/shard_map/ppermute | solution.py:258
  57.2 3.5 %collective-permute-start.12 = (f32[1032,128]{1,0:T(8,128)S(1)}, f32[1032,128]{1,0:T(8,128)S(1)}, u32[]{:S(2)}, u32[]{:S(2)}) collective-permute-start(f32[1032,128]{1,0:T(8,128)S(1)} %collective-permute-done.11.refs_0_), channel_id=1, source_target_pairs={{0,2},{2,0},{4,6},{6,4},{8,10},{10,8},{12,14},{14,12},{16,18},{18,... | collective-permute-start | bytes 1585160 | tf_op jit(solution)/shard_map/ppermute | solution.py:258
  57.9 7.0 %collective-permute-start.14 = (f32[1032,128]{1,0:T(8,128)S(1)}, f32[1032,128]{1,0:T(8,128)S(1)}, u32[]{:S(2)}, u32[]{:S(2)}) collective-permute-start(f32[1032,128]{1,0:T(8,128)S(1)} %collective-permute-done.6.refs_0_), channel_id=1, source_target_pairs={{0,2},{2,0},{4,6},{6,4},{8,10},{10,8},{12,14},{14,12},{16,18},{18,... | collective-permute-start | bytes 1585160 | tf_op jit(solution)/shard_map/ppermute | solution.py:258
  58.1 10.7 %collective-permute-start.10 = (f32[1032,128]{1,0:T(8,128)S(1)}, f32[1032,128]{1,0:T(8,128)S(1)}, u32[]{:S(2)}, u32[]{:S(2)}) collective-permute-start(f32[1032,128]{1,0:T(8,128)S(1)} %collective-permute-done.6.refs_0_), channel_id=1, source_target_pairs={{0,28},{2,34},{4,0},{6,38},{8,4},{10,42},{12,8},{14,46},{16,12},{1... | collective-permute-start | bytes 1585160 | tf_op jit(solution)/shard_map/ppermute | solution.py:258
  60.7 9.7 %collective-permute-start.13 = (f32[1032,128]{1,0:T(8,128)S(1)}, f32[1032,128]{1,0:T(8,128)S(1)}, u32[]{:S(2)}, u32[]{:S(2)}) collective-permute-start(f32[1032,128]{1,0:T(8,128)S(1)} %collective-permute-done.12.refs_1_), channel_id=1, source_target_pairs={{0,64},{2,6},{4,68},{6,10},{8,72},{10,14},{12,76},{14,18},{16,80},... | collective-permute-start | bytes 1585160 | tf_op jit(solution)/shard_map/ppermute | solution.py:258
